TPU v7x, 512 devices: a whole 4x4x16 slice. The times are simulated.
512 devices in a mesh: row: 16 (over y, x), col: 32 (over z, core).
Axes of the slice: x: 4, y: 4, z: 16, core: 2. Of those that a mesh axis runs over, the one named last changes fastest.
Arguments:
- inputs: bfloat16 [1024, 12288], P('col', 'row'), may hold values from -6 to 6
- out_grad: bfloat16 [1024, 24576], P('row', 'col'), may hold values from -6 to 6
- preact: bfloat16 [1024, 24576], P('row', 'col'), may hold values from -5 to 5
- weight: bfloat16 [12288, 24576], P('row', 'col'), may hold values from -0.0546875 to 0.0546875
Outputs:
- input_grad: bfloat16 [1024, 12288], P('col', 'row')
- weight_grad: bfloat16 [12288, 24576], P('row', 'col')
All inputs are finite; a program needn't handle non-finite values.
Results may differ from a plain program's by a relative error of at most 0.0049.
Values may be sent and summed in bfloat16 or wider, within the bound.
No kernel may reach another device: no remote copies, remote signals or barrier semaphores. Data moves between devices by JAX's collectives and lax.ppermute only.
A program may use at most 64 MiB of HBM per device.

v0:
```python
import jax
import jax.numpy as jnp
from jax import lax
from jax.sharding import PartitionSpec as P


def activation_grad(out_grad, preact):
    value = preact.astype(jnp.float32)
    cdf = 0.5 * (1.0 + jax.scipy.special.erf(value * 0.7071067811865476))
    pdf = jnp.exp(-0.5 * value * value) * 0.3989422804014327
    return (out_grad.astype(jnp.float32) * (cdf + value * pdf)).astype(jnp.bfloat16)


def on_device(inputs, out_grad, preact, weight):
    grad_all, preact_all = (
        lax.all_gather(out_grad, "row", axis=0, tiled=True),
        lax.all_gather(preact, "row", axis=0, tiled=True),
    )
    act_grad = activation_grad(grad_all, preact_all)
    input_all = lax.all_gather(inputs, "col", axis=0, tiled=True)
    total_tokens = input_all.shape[0]
    weight_sum = lax.dot_general(
        input_all, act_grad, (((0,), (0,)), ((), ())), preferred_element_type=jnp.float32
    )
    weight_grad = (weight_sum * total_tokens ** (-0.5)).astype(jnp.bfloat16)
    terms = lax.dot_general(
        act_grad, weight, (((1,), (1,)), ((), ())), preferred_element_type=jnp.float32
    )
    summed = lax.psum_scatter(terms, "col", scatter_dimension=0, tiled=True)
    return (summed.astype(jnp.bfloat16), weight_grad)


def solution(mesh):
    return jax.shard_map(
        on_device,
        mesh=mesh,
        in_specs=(P("col", "row"), P("row", "col"), P("row", "col"), P("row", "col")),
        out_specs=(P("col", "row"), P("row", "col")),
        check_vma=False,
    )
```

profile of v0, /device:TPU:8, one launch (start us, length us, event | category | flops | bytes accessed | tf_op | source)
XLA Modules:
  0.0 329.1 jit_solution(18240139612966488515)
XLA Ops:
  7.2 0.0 copy-start
  7.2 0.0 all-gather.4.cloned.1.call-start
  7.2 0.7 all-gather.4.cloned.1.call-update
  7.9 0.0 all-gather.6.cloned.1.call-start
  8.0 0.7 all-gather.6.cloned.1.call-update
  8.7 0.0 all-gather.8.cloned.1.call-start
  8.7 0.7 all-gather.8.cloned.1.call-update
  9.4 0.0 reduce-scatter.2.cloned.1.call-start
  9.4 64.8 %all-gather.4.cloned.1.call-done = bf16[1024,768]{1,0:T(8,128)(2,1)} async-done(((bf16[64,768]{1,0:T(8,128)(2,1)}), bf16[1024,768]{1,0:T(8,128)(2,1)}) %all-gather.4.cloned.1.call-update) | async-done | bytes 1572880 | tf_op jit(solution)/shard_map/all_gather | solution.py:16
  74.3 61.8 %all-gather.6.cloned.1.call-done = bf16[1024,768]{1,0:T(8,128)(2,1)} async-done(((bf16[64,768]{1,0:T(8,128)(2,1)}), bf16[1024,768]{1,0:T(8,128)(2,1)}) %all-gather.6.cloned.1.call-update) | async-done | bytes 1572880 | tf_op jit(solution)/shard_map/all_gather | solution.py:17
  136.0 2.9 fusion.7
  138.9 0.0 copy-done
  139.0 3.1 fusion.9
  142.0 0.0 reduce-scatter.2.cloned.1.call-update
  142.0 67.4 %all-gather.8.cloned.1.call-done = bf16[1024,768]{1,0:T(8,128)(2,1)} async-done(((bf16[32,768]{1,0:T(8,128)(2,1)}), bf16[1024,768]{1,0:T(8,128)(2,1)}) %all-gather.8.cloned.1.call-update) | async-done | bytes 1572880 | tf_op jit(solution)/shard_map/all_gather | solution.py:20
  209.4 3.9 %fusion.8 = bf16[768,768]{0,1:T(8,128)(2,1)} fusion(bf16[1024,768]{1,0:T(8,128)(2,1)S(1)} %fusion.7, bf16[1024,768]{1,0:T(8,128)(2,1)} %all-gather.8.cloned.1.call-done), kind=kOutput, calls=%fused_computation.13 | convolution fusion | flops 1209139200 | bytes 4325376 | tf_op jit(solution)/shard_map/dot_general | solution.py:22
  213.3 2.4 copy.6
  215.7 105.3 %reduce-scatter.2.cloned.1.call-done = f32[32,768]{1,0:T(8,128)} async-done(((f32[1024,768]{1,0:T(8,128)}), f32[32,768]{1,0:T(8,128)}) %reduce-scatter.2.cloned.1.call-update) | async-done | bytes 98320 | tf_op jit(solution)/shard_map/reduce_scatter | solution.py:29
  321.1 1.5 convert_element_type.21
Async XLA Ops:
  7.2 131.8 %copy-start = (bf16[768,768]{1,0:T(8,128)(2,1)S(1)}, bf16[768,768]{1,0:T(8,128)(2,1)}, u32[]{:S(2)}) copy-start(bf16[768,768]{1,0:T(8,128)(2,1)} %param.7) | copy-start | bytes 3538948
  7.2 67.1 %all-gather.4.cloned.1.call-start = ((), (), s32[]{:S(2)}) async-start(), calls=%async_computation.1 | async-start | bytes 1671168 | tf_op jit(solution)/shard_map/all_gather | solution.py:16
  7.9 128.1 %all-gather.6.cloned.1.call-start = ((), (), s32[]{:S(2)}) async-start(), calls=%async_computation.2 | async-start | bytes 1671168 | tf_op jit(solution)/shard_map/all_gather | solution.py:17
  8.7 200.8 %all-gather.8.cloned.1.call-start = ((), (), s32[]{:S(2)}) async-start(), calls=%async_computation.4 | async-start | bytes 1622016 | tf_op jit(solution)/shard_map/all_gather | solution.py:20
  9.4 311.7 %reduce-scatter.2.cloned.1.call-start = ((), (), s32[]{:S(2)}) async-start(), calls=%async_computation.3 | async-start | bytes 3244032 | tf_op jit(solution)/shard_map/reduce_scatter | solution.py:29
Sparse Core Ops, SparseCore 0:
  11.0 63.2 all-gather.3
  77.3 58.7 all-gather.5
  138.2 71.2 all-gather.7
  212.1 108.9 reduce-scatter.1
where the time goes:
time: 329 us
  waiting for transfers between devices  301 us (91%)
  between operations  13.8 us (4%)
  matrix products  6.97 us (2%)
  other arithmetic  4.4 us (1%)
    reduce_scatter x1, waiting for transfers between devices, on_device(): summed = lax.psum_scatter(terms, 'col', scatter_dimension=0, tiled=True)  105 us
    all_gather x1, waiting for transfers between devices, on_device(): input_all = lax.all_gather(inputs, 'col', axis=0, tiled=True)  67.4 us
    all_gather x1, waiting for transfers between devices, on_device(): lax.all_gather(out_grad, 'row', axis=0, tiled=True)  64.8 us
    all_gather x1, waiting for transfers between devices, on_device(): lax.all_gather(preact, 'row', axis=0, tiled=True)  61.8 us
  transfers between devices with their start and end apart: 4, of which 4 were waited for; matrix products, arithmetic and copies ran while one was open for 4% of the time, Pallas kernels for 0%

commit v1 on v0

v1 whole, which is shorter than its diff:
```python
import jax
import jax.numpy as jnp
from jax import lax
from jax.sharding import Mesh, PartitionSpec as P


def activation_grad(out_grad, preact):
    value = preact.astype(jnp.float32)
    cdf = 0.5 * (1.0 + jax.scipy.special.erf(value * 0.7071067811865476))
    pdf = jnp.exp(-0.5 * value * value) * 0.3989422804014327
    return (out_grad.astype(jnp.float32) * (cdf + value * pdf)).astype(jnp.bfloat16)


def on_device(inputs, out_grad, preact, weight):
    core = lax.axis_index("core")
    swap = [(0, 1), (1, 0)]
    input_all = lax.all_gather(inputs, ("z", "core"), axis=0, tiled=True)
    weight_other = lax.ppermute(weight, "core", swap)

    act = lax.optimization_barrier(activation_grad(out_grad, preact))
    copies = jnp.broadcast_to(act[None], (16,) + act.shape)
    act_all = lax.all_to_all(copies, ("y", "x"), 0, 0, tiled=True)
    tokens = 16 * act.shape[0]
    per = act_all.reshape(16, 2, tokens // 32, act.shape[1])
    mine = lax.dynamic_index_in_dim(per, core, 1, keepdims=False).reshape(tokens // 2, -1)
    theirs = lax.dynamic_index_in_dim(per, 1 - core, 1, keepdims=False).reshape(tokens // 2, -1)
    got = lax.ppermute(theirs, "core", swap)
    dims = (((1,), (1,)), ((), ()))
    terms = lax.dot_general(mine, weight, dims, preferred_element_type=jnp.float32)
    terms = terms + lax.dot_general(got, weight_other, dims, preferred_element_type=jnp.float32)
    sent = terms.astype(jnp.bfloat16)
    parts = lax.all_to_all(sent.reshape(16, tokens // 32, -1), "z", 0, 0, tiled=True)
    input_grad = jnp.sum(parts.astype(jnp.float32), axis=0).astype(jnp.bfloat16)

    weight_sum = lax.dot_general(
        input_all, act_all.reshape(tokens, -1), (((0,), (0,)), ((), ())), preferred_element_type=jnp.float32
    )
    weight_grad = (weight_sum * tokens ** (-0.5)).astype(jnp.bfloat16)
    return input_grad, weight_grad


def solution(mesh):
    fine = Mesh(mesh.devices.reshape(4, 4, 16, 2), ("y", "x", "z", "core"))
    across, along = ("y", "x"), ("z", "core")
    return jax.shard_map(
        on_device,
        mesh=fine,
        in_specs=(P(along, across), P(across, along), P(across, along), P(across, along)),
        out_specs=(P(along, across), P(across, along)),
        check_vma=False,
    )
```

time: 329 us -> 144 us (0.44)
  the two profiles are of different devices: /device:TPU:8 before, /device:TPU:47 now
where the time goes in v1:
time: 144 us; the launch traced here: 143 us
  waiting for transfers between devices  87.2 us (61%)
  starting transfers between devices  29 us (20%)
  between operations  14.1 us (10%)
  matrix products  8.15 us (6%)
  local copies, waits for them, and re-layouts  2.87 us (2%)
  other arithmetic  1.77 us (1%)
    all_gather x1, waiting for transfers between devices, on_device(): input_all = lax.all_gather(inputs, ('z', 'core'), axis=0, tiled=True)  71.4 us
    all_to_all x1, waiting for transfers between devices, on_device(): act_all = lax.all_to_all(copies, ('y', 'x'), 0, 0, tiled=True)  15.8 us
    all_to_all x1, starting transfers between devices, on_device(): lax.all_to_all(sent.reshape(16, tokens // 32, -1), 'z', 0, 0, tiled=True)  14.7 us
    all_to_all x1, starting transfers between devices, on_device(): act_all = lax.all_to_all(copies, ('y', 'x'), 0, 0, tiled=True)  6.75 us
    ppermute x1, starting transfers between devices, on_device(): got = lax.ppermute(theirs, 'core', swap)  4.46 us
    dot_general x1, matrix products, on_device(): lax.dot_general(got, weight_other, dims, preferred_element_type=jnp.float32)  3.22 us
    ppermute x1, starting transfers between devices, on_device(): weight_other = lax.ppermute(weight, 'core', swap)  3.15 us
  transfers between devices with their start and end apart: 5, of which 2 were waited for; matrix products, arithmetic and copies ran while one was open for 7% of the time, Pallas kernels for 0%

profile of v1, /device:TPU:47, one launch (start us, length us, event | category | flops | bytes accessed | tf_op | source)
XLA Modules:
  0.0 143.1 jit_solution(4047259951767631232)
XLA Ops:
  7.2 1.0 fusion.8
  8.2 1.3 broadcast_in_dim.2
  9.5 6.7 %all-to-all-start = ((bf16[16,64,768]{2,1,0:T(8,128)(2,1)}), bf16[16,64,768]{2,1,0:T(8,128)(2,1)S(1)}, u32[]{:S(2)}, u32[]{:S(2)}) async-start(bf16[16,64,768]{2,1,0:T(8,128)(2,1)} %broadcast_in_dim.2), calls=%async_computation | async-start | bytes 3145728 | tf_op jit(solution)/shard_map/all_to_all | solution.py:22
  16.3 0.0 all-gather.2.cloned.1.call-start
  16.3 3.1 %collective-permute-start.1 = (bf16[768,768]{1,0:T(8,128)(2,1)}, bf16[768,768]{1,0:T(8,128)(2,1)}, u32[]{:S(2)}, u32[]{:S(2)}) collective-permute-start(bf16[768,768]{1,0:T(8,128)(2,1)} %param.7), channel_id=1, source_target_pairs={{0,1},{1,0},{2,3},{3,2},{4,5},{5,4},{6,7},{7,6},{8,9},{9,8},{10,11... | collective-permute-start | bytes 3538952 | tf_op jit(solution)/shard_map/ppermute | solution.py:18
  19.5 15.8 %all-to-all-done = bf16[16,64,768]{2,1,0:T(8,128)(2,1)S(1)} async-done(((bf16[16,64,768]{2,1,0:T(8,128)(2,1)}), bf16[16,64,768]{2,1,0:T(8,128)(2,1)S(1)}, u32[]{:S(2)}, u32[]{:S(2)}) %all-to-all-start) | async-done | bytes 1572896 | tf_op jit(solution)/shard_map/all_to_all | solution.py:22
  35.2 0.1 constant_dynamic-slice_fusion
  35.3 4.5 %collective-permute-start = (bf16[512,768]{1,0:T(8,128)(2,1)S(1)}, bf16[512,768]{1,0:T(8,128)(2,1)}, u32[]{:S(2)}, u32[]{:S(2)}) collective-permute-start(bf16[512,768]{1,0:T(8,128)(2,1)S(1)} %bitcast.15), channel_id=1, source_target_pairs={{0,1},{1,0},{2,3},{3,2},{4,5},{5,4},{6,7},{7,6},{8,9},{9,8},{10,11... | collective-permute-start | bytes 2359304 | tf_op jit(solution)/shard_map/ppermute | solution.py:27
  39.8 0.0 all-gather.2.cloned.1.call-update
  39.8 2.1 %fusion.9 = f32[512,768]{1,0:T(8,128)S(1)} fusion(bf16[512,768]{1,0:T(8,128)(2,1)S(1)} %bitcast.16, bf16[768,768]{1,0:T(8,128)(2,1)} %param.7), kind=kOutput, calls=%fused_computation.17 | convolution fusion | flops 603979776 | bytes 3538944 | tf_op jit(solution)/shard_map/dot_general | solution.py:29
  41.9 0.0 collective-permute-done.1
  41.9 0.0 collective-permute-done
  42.0 3.2 %add_convert_fusion = bf16[512,768]{1,0:T(8,128)(2,1)} fusion(f32[512,768]{1,0:T(8,128)S(1)} %fusion.9, bf16[512,768]{1,0:T(8,128)(2,1)} %collective-permute-done, bf16[768,768]{1,0:T(8,128)(2,1)} %collective-permute-done.1), kind=kOutput, calls=%fused_computation.1 | convolution fusion | flops 604766208 | bytes 4325376 | tf_op jit(solution)/shard_map/dot_general | solution.py:30
  45.2 14.7 %all-to-all-start.1 = ((bf16[16,32,768]{2,1,0:T(8,128)(2,1)}), bf16[16,32,768]{2,1,0:T(8,128)(2,1)S(1)}, u32[]{:S(2)}, u32[]{:S(2)}) async-start(bf16[16,32,768]{2,1,0:T(8,128)(2,1)} %bitcast.3), calls=%async_computation.1 | async-start | bytes 1572864 | tf_op jit(solution)/shard_map/all_to_all | solution.py:32
  59.8 71.4 %all-gather.2.cloned.1.call-done = bf16[1024,768]{1,0:T(8,128)(2,1)} async-done(((bf16[32,768]{1,0:T(8,128)(2,1)}), bf16[1024,768]{1,0:T(8,128)(2,1)}) %all-gather.2.cloned.1.call-update) | async-done | bytes 1572880 | tf_op jit(solution)/shard_map/all_gather | solution.py:17
  131.2 2.8 %fusion = bf16[768,768]{0,1:T(8,128)(2,1)S(1)} fusion(bf16[1024,768]{1,0:T(8,128)(2,1)S(1)} %bitcast.14, bf16[1024,768]{1,0:T(8,128)(2,1)} %all-gather.2.cloned.1.call-done), kind=kOutput, calls=%fused_computation.2 | convolution fusion | flops 1209139200 | bytes 4325376 | tf_op jit(solution)/shard_map/dot_general | solution.py:35
  134.1 1.5 %copy.6 = bf16[768,768]{1,0:T(8,128)(2,1)} copy(bf16[768,768]{0,1:T(8,128)(2,1)S(1)} %fusion) | data formatting | bytes 2359296
  135.6 0.0 all-to-all-done.1
  135.6 0.7 reduce_sum.12
Async XLA Ops:
  9.5 25.7 %all-to-all-start = ((bf16[16,64,768]{2,1,0:T(8,128)(2,1)}), bf16[16,64,768]{2,1,0:T(8,128)(2,1)S(1)}, u32[]{:S(2)}, u32[]{:S(2)}) async-start(bf16[16,64,768]{2,1,0:T(8,128)(2,1)} %broadcast_in_dim.2), calls=%async_computation | async-start | bytes 3145728 | tf_op jit(solution)/shard_map/all_to_all | solution.py:22
  16.3 115.0 %all-gather.2.cloned.1.call-start = ((), (), s32[]{:S(2)}) async-start(), calls=%async_computation.2 | async-start | bytes 1622016 | tf_op jit(solution)/shard_map/all_gather | solution.py:17
  16.3 25.6 %collective-permute-start.1 = (bf16[768,768]{1,0:T(8,128)(2,1)}, bf16[768,768]{1,0:T(8,128)(2,1)}, u32[]{:S(2)}, u32[]{:S(2)}) collective-permute-start(bf16[768,768]{1,0:T(8,128)(2,1)} %param.7), channel_id=1, source_target_pairs={{0,1},{1,0},{2,3},{3,2},{4,5},{5,4},{6,7},{7,6},{8,9},{9,8},{10,11... | collective-permute-start | bytes 3538952 | tf_op jit(solution)/shard_map/ppermute | solution.py:18
  35.3 6.6 %collective-permute-start = (bf16[512,768]{1,0:T(8,128)(2,1)S(1)}, bf16[512,768]{1,0:T(8,128)(2,1)}, u32[]{:S(2)}, u32[]{:S(2)}) collective-permute-start(bf16[512,768]{1,0:T(8,128)(2,1)S(1)} %bitcast.15), channel_id=1, source_target_pairs={{0,1},{1,0},{2,3},{3,2},{4,5},{5,4},{6,7},{7,6},{8,9},{9,8},{10,11... | collective-permute-start | bytes 2359304 | tf_op jit(solution)/shard_map/ppermute | solution.py:27
  45.2 90.4 %all-to-all-start.1 = ((bf16[16,32,768]{2,1,0:T(8,128)(2,1)}), bf16[16,32,768]{2,1,0:T(8,128)(2,1)S(1)}, u32[]{:S(2)}, u32[]{:S(2)}) async-start(bf16[16,32,768]{2,1,0:T(8,128)(2,1)} %bitcast.3), calls=%async_computation.1 | async-start | bytes 1572864 | tf_op jit(solution)/shard_map/all_to_all | solution.py:32
Sparse Core Ops, SparseCore 0:
  40.0 91.2 all-gather.1

commit v2 on v1

v2 whole, which is shorter than its diff:
```python
import jax
import jax.numpy as jnp
from jax import lax
from jax.experimental import pallas as pl
from jax.experimental.pallas import tpu as pltpu
from jax.sharding import Mesh, PartitionSpec as P

DEPTH = 16
SWAP = [(0, 1), (1, 0)]
PARITIES = [list(range(0, DEPTH, 2)), list(range(1, DEPTH, 2))]


def activation_grad(out_grad, preact):
    value = preact.astype(jnp.float32)
    cdf = 0.5 * (1.0 + jax.scipy.special.erf(value * 0.7071067811865476))
    pdf = jnp.exp(-0.5 * value * value) * 0.3989422804014327
    return (out_grad.astype(jnp.float32) * (cdf + value * pdf)).astype(jnp.bfloat16)


def hop(x, step):
    pairs = []
    for z in range(DEPTH):
        pairs.append((2 * z, 2 * ((z + step) % DEPTH)))
        pairs.append((2 * z + 1, 2 * ((z - step) % DEPTH) + 1))
    return lax.ppermute(x, ("z", "core"), pairs)


def place(rows, at_ref, held, last, out):
    for j in range(DEPTH):
        source, i = (held, j) if j < DEPTH // 2 else (last, j - DEPTH // 2)
        at = pl.multiple_of(at_ref[j] * rows, rows)
        out[pl.ds(at, rows), :] = source[i * rows : (i + 1) * rows, :]


def placed(at, held, last):
    rows, width = held.shape[0] * 2 // DEPTH, held.shape[1]
    whole = pl.BlockSpec(memory_space=pltpu.VMEM)
    return pl.pallas_call(
        lambda *refs: place(rows, *refs),
        out_shape=jax.ShapeDtypeStruct((DEPTH * rows, width), held.dtype),
        in_specs=[pl.BlockSpec(memory_space=pltpu.SMEM)] + [whole] * 2,
        out_specs=whole,
        cost_estimate=pl.CostEstimate(flops=0, bytes_accessed=1, transcendentals=0),
    )(at, held, last)


def on_device(inputs, out_grad, preact, weight):
    core, z = lax.axis_index("core"), lax.axis_index("z")
    rows, width = inputs.shape[0], weight.shape[1]
    scale = (2 * DEPTH * rows) ** (-0.5)

    def act_of(which):
        part = [lax.dynamic_slice(a, (which * rows, 0), (rows, width)) for a in (out_grad, preact)]
        return activation_grad(*part)

    other = lax.ppermute(lax.optimization_barrier(act_of(1 - core)), "core", SWAP)
    pair = jnp.stack([act_of(core), other])
    copies = lax.optimization_barrier(jnp.broadcast_to(pair[None], (DEPTH,) + pair.shape))
    copies, inputs, weight_sent = lax.optimization_barrier((copies, inputs, weight))
    arrived = lax.all_to_all(copies, ("y", "x"), 0, 0, tiled=True)
    weight_other = lax.ppermute(weight_sent, "core", SWAP)
    held = jnp.concatenate([inputs, hop(inputs, 8)], axis=0)
    held = jnp.concatenate([held, hop(held, 4)], axis=0)

    per = arrived.reshape(DEPTH // 2, 2, 2, rows, width)
    near = z % 2

    def products(parity):
        part = lax.dynamic_slice(per, (0, parity, 0, 0, 0), (DEPTH // 2, 1, 2, rows, width))
        dims = (((1,), (1,)), ((), ()))
        own, theirs = part[:, 0, 0].reshape(-1, width), part[:, 0, 1].reshape(-1, width)
        total = lax.dot_general(own, weight, dims, preferred_element_type=jnp.float32)
        return total + lax.dot_general(theirs, weight_other, dims, preferred_element_type=jnp.float32)

    held, per = lax.optimization_barrier((held, per))
    third = hop(held, 2)
    far = products(1 - near).astype(jnp.bfloat16)
    below = hop(far, 1)
    total = products(near)
    held = jnp.concatenate([held, third], axis=0)
    last = hop(held, 1)
    total = total + below.astype(jnp.float32)
    sent = total.astype(jnp.bfloat16).reshape(DEPTH // 2, rows, -1)
    parts = lax.all_to_all(sent, "z", 0, 0, axis_index_groups=PARITIES, tiled=True)

    turn = jnp.array([int(f"{j:04b}"[::-1], 2) for j in range(DEPTH)], jnp.int32)
    at = (z - (1 - 2 * core) * turn + DEPTH) % DEPTH
    input_mine = placed(at, held, last)
    act_own = arrived[:, 0].reshape(DEPTH * rows, width)
    act_other = arrived[:, 1].reshape(DEPTH * rows, width)
    dims = (((0,), (0,)), ((), ()))
    for_other = lax.dot_general(input_mine, act_other, dims, preferred_element_type=jnp.float32)
    from_other = lax.ppermute((for_other * scale).astype(jnp.bfloat16), "core", SWAP)
    weight_sum = lax.dot_general(input_mine, act_own, dims, preferred_element_type=jnp.float32)
    weight_grad = (weight_sum * scale + from_other.astype(jnp.float32)).astype(jnp.bfloat16)
    input_grad = jnp.sum(parts.astype(jnp.float32), axis=0).astype(jnp.bfloat16)
    return input_grad, weight_grad


def solution(mesh):
    fine = Mesh(mesh.devices.reshape(4, 4, DEPTH, 2), ("y", "x", "z", "core"))
    across, along = ("y", "x"), ("z", "core")
    return jax.shard_map(
        on_device,
        mesh=fine,
        in_specs=(P(along, across), P(across, along), P(across, along), P(across, along)),
        out_specs=(P(along, across), P(across, along)),
        check_vma=False,
    )
```

time: 144 us -> 105 us (0.73)
  the two profiles are of different devices: /device:TPU:47 before, /device:TPU:2 now
where the time goes in v2:
time: 105 us; the launch traced here: 104 us
  starting transfers between devices  56.9 us (54%)
  waiting for transfers between devices  27.7 us (26%)
  matrix products  9.2 us (9%)
  other arithmetic  4.76 us (5%)
  local copies, waits for them, and re-layouts  2.53 us (2%)
  Pallas kernels  2.07 us (2%)
    ppermute x5, starting transfers between devices, hop(): return lax.ppermute(x, ('z', 'core'), pairs)  31.6 us
    all_to_all x1, waiting for transfers between devices, on_device(): lax.all_to_all(sent, 'z', 0, 0, axis_index_groups=PARITIES, tiled=True)  14.2 us
    ppermute x5, waiting for transfers between devices, hop(): return lax.ppermute(x, ('z', 'core'), pairs)  12.3 us
    all_to_all x1, starting transfers between devices, on_device(): lax.all_to_all(sent, 'z', 0, 0, axis_index_groups=PARITIES, tiled=True)  10 us
    all_to_all x1, starting transfers between devices, on_device(): arrived = lax.all_to_all(copies, ('y', 'x'), 0, 0, tiled=True)  9.53 us
    dot_general x2, matrix products, products(): lax.dot_general(theirs, weight_other, dims, preferred_element_type=jnp.fl...  4.34 us
    dot_general x1, matrix products, on_device(): lax.dot_general(input_mine, act_other, dims, preferred_element_type=jnp.f...  3.03 us
    convert_element_type x1, other arithmetic, on_device(): (weight_sum * scale + from_other.astype(jnp.float32)).astype(jnp.bfloat16)  2.55 us
  transfers between devices with their start and end apart: 10, of which 6 were waited for; matrix products, arithmetic and copies ran while one was open for 11% of the time, Pallas kernels for 2%

profile of v2, /device:TPU:2, one launch (start us, length us, event | category | flops | bytes accessed | tf_op | source)
XLA Modules:
  0.0 104.0 jit_solution(2929836679866785009)
XLA Ops:
  0.6 1.0 fusion.19
  1.6 1.9 %collective-permute-start = (bf16[32,768]{1,0:T(8,128)(2,1)S(1)}, bf16[32,768]{1,0:T(8,128)(2,1)S(1)}, u32[]{:S(2)}, u32[]{:S(2)}) collective-permute-start(bf16[32,768]{1,0:T(8,128)(2,1)S(1)} %get-tuple-element.19), channel_id=1, source_target_pairs={{0,1},{1,0},{2,3},{3,2},{4,5},{5,4},{6,7},{7,6},{8,9},{9,8},{10,11... | collective-permute-start | bytes 147464 | tf_op jit(solution)/shard_map/ppermute | solution.py:56
  3.5 1.2 %collective-permute-done = bf16[32,768]{1,0:T(8,128)(2,1)S(1)} collective-permute-done((bf16[32,768]{1,0:T(8,128)(2,1)S(1)}, bf16[32,768]{1,0:T(8,128)(2,1)S(1)}, u32[]{:S(2)}, u32[]{:S(2)}) %collective-permute-start) | collective-permute-done | bytes 49184 | tf_op jit(solution)/shard_map/ppermute | solution.py:56
  4.8 1.4 %broadcast_in_dim.2 = bf16[16,2,32,768]{3,2,1,0:T(8,128)(2,1)} broadcast(bf16[2,32,768]{2,1,0:T(8,128)(2,1)S(1)} %pad_maximum_fusion.1), dimensions={1,2,3} | broadcast | bytes 1671168 | tf_op jit(solution)/shard_map/broadcast_in_dim | solution.py:58
  6.1 9.5 %all-to-all-start = ((bf16[16,2,32,768]{3,2,1,0:T(8,128)(2,1)}), bf16[16,2,32,768]{3,2,1,0:T(8,128)(2,1)S(1)}, u32[]{:S(2)}, u32[]{:S(2)}) async-start(bf16[16,2,32,768]{3,2,1,0:T(8,128)(2,1)} %broadcast_in_dim.2), calls=%async_computation | async-start | bytes 3145728 | tf_op jit(solution)/shard_map/all_to_all | solution.py:60
  15.7 1.9 %collective-permute-start.3 = (bf16[768,768]{1,0:T(8,128)(2,1)S(1)}, bf16[768,768]{1,0:T(8,128)(2,1)}, u32[]{:S(2)}, u32[]{:S(2)}) collective-permute-start(bf16[768,768]{1,0:T(8,128)(2,1)S(1)} %copy-done.1), channel_id=1, source_target_pairs={{0,1},{1,0},{2,3},{3,2},{4,5},{5,4},{6,7},{7,6},{8,9},{9,8},{10,11... | collective-permute-start | bytes 3538952 | tf_op jit(solution)/shard_map/ppermute | solution.py:61
  17.6 13.8 %collective-permute-start.1 = (bf16[32,768]{1,0:T(8,128)(2,1)S(1)}, bf16[32,768]{1,0:T(8,128)(2,1)S(1)}, u32[]{:S(2)}, u32[]{:S(2)}) collective-permute-start(bf16[32,768]{1,0:T(8,128)(2,1)S(1)} %copy-done.4), channel_id=1, source_target_pairs={{0,16},{1,17},{2,18},{3,19},{4,20},{5,21},{6,22},{7,23},{8,24},{9,... | collective-permute-start | bytes 147464 | tf_op jit(solution)/shard_map/ppermute | solution.py:25
  31.4 2.7 %collective-permute-done.1 = bf16[32,768]{1,0:T(8,128)(2,1)S(1)} collective-permute-done((bf16[32,768]{1,0:T(8,128)(2,1)S(1)}, bf16[32,768]{1,0:T(8,128)(2,1)S(1)}, u32[]{:S(2)}, u32[]{:S(2)}) %collective-permute-start.1) | collective-permute-done | bytes 49184 | tf_op jit(solution)/shard_map/ppermute | solution.py:25
  34.1 7.7 %collective-permute-start.2 = (bf16[64,768]{1,0:T(8,128)(2,1)S(1)}, bf16[64,768]{1,0:T(8,128)(2,1)S(1)}, u32[]{:S(2)}, u32[]{:S(2)}) collective-permute-start(bf16[64,768]{1,0:T(8,128)(2,1)S(1)} %pad_maximum_fusion.2), channel_id=1, source_target_pairs={{0,8},{1,25},{2,10},{3,27},{4,12},{5,29},{6,14},{7,31},{8,16},{9,1... | collective-permute-start | bytes 294920 | tf_op jit(solution)/shard_map/ppermute | solution.py:25
  42.3 3.7 %collective-permute-done.2 = bf16[64,768]{1,0:T(8,128)(2,1)S(1)} collective-permute-done((bf16[64,768]{1,0:T(8,128)(2,1)S(1)}, bf16[64,768]{1,0:T(8,128)(2,1)S(1)}, u32[]{:S(2)}, u32[]{:S(2)}) %collective-permute-start.2) | collective-permute-done | bytes 98336 | tf_op jit(solution)/shard_map/ppermute | solution.py:25
  46.0 6.2 %collective-permute-start.5 = (bf16[128,768]{1,0:T(8,128)(2,1)S(1)}, bf16[128,768]{1,0:T(8,128)(2,1)S(1)}, u32[]{:S(2)}, u32[]{:S(2)}) collective-permute-start(bf16[128,768]{1,0:T(8,128)(2,1)S(1)} %pad_maximum_fusion), channel_id=1, source_target_pairs={{0,4},{1,29},{2,6},{3,31},{4,8},{5,1},{6,10},{7,3},{8,12},{9,5},{1... | collective-permute-start | bytes 589832 | tf_op jit(solution)/shard_map/ppermute | solution.py:25
  52.9 1.8 %fusion.2 = bf16[256,768]{1,0:T(8,128)(2,1)S(1)} fusion(f32[256,768]{1,0:T(8,128)S(1)} %fusion.23, bf16[256,768]{1,0:T(8,128)(2,1)S(1)} %bitcast.28, bf16[768,768]{1,0:T(8,128)(2,1)} %collective-permute-done.3), kind=kOutput, calls=%fused_computation.6 | convolution fusion | flops 302383104 | bytes 2752512 | tf_op jit(solution)/shard_map/dot_general | solution.py:73
  55.2 1.9 %collective-permute-start.4 = (bf16[256,768]{1,0:T(8,128)(2,1)S(1)}, bf16[256,768]{1,0:T(8,128)(2,1)S(1)}, u32[]{:S(2)}, u32[]{:S(2)}) collective-permute-start(bf16[256,768]{1,0:T(8,128)(2,1)S(1)} %fusion.2), channel_id=1, source_target_pairs={{0,2},{1,31},{2,4},{3,1},{4,6},{5,3},{6,8},{7,5},{8,10},{9,7},{10,... | collective-permute-start | bytes 1179656 | tf_op jit(solution)/shard_map/ppermute | solution.py:25
  57.2 3.4 %collective-permute-done.5 = bf16[128,768]{1,0:T(8,128)(2,1)S(1)} collective-permute-done((bf16[128,768]{1,0:T(8,128)(2,1)S(1)}, bf16[128,768]{1,0:T(8,128)(2,1)S(1)}, u32[]{:S(2)}, u32[]{:S(2)}) %collective-permute-start.5) | collective-permute-done | bytes 196640 | tf_op jit(solution)/shard_map/ppermute | solution.py:25
  60.7 1.9 %collective-permute-start.6 = (bf16[256,768]{1,0:T(8,128)(2,1)S(1)}, bf16[256,768]{1,0:T(8,128)(2,1)}, u32[]{:S(2)}, u32[]{:S(2)}) collective-permute-start(bf16[256,768]{1,0:T(8,128)(2,1)S(1)} %constant_dynamic-update-slice_fusion.refs_1_), channel_id=1, source_target_pairs={{0,2},{1,31},{2,4},{3,1},{4,6},{5,3},{6,8},{7,5},{8,10},{9,7},{10,... | collective-permute-start | bytes 1179656 | tf_op jit(solution)/shard_map/ppermute | solution.py:25
  62.6 1.0 fusion.21
  63.6 2.5 %collective-permute-done.4 = bf16[256,768]{1,0:T(8,128)(2,1)S(1)} collective-permute-done((bf16[256,768]{1,0:T(8,128)(2,1)S(1)}, bf16[256,768]{1,0:T(8,128)(2,1)S(1)}, u32[]{:S(2)}, u32[]{:S(2)}) %collective-permute-start.4) | collective-permute-done | bytes 393248 | tf_op jit(solution)/shard_map/ppermute | solution.py:25
  66.1 2.6 %fusion.1 = bf16[256,768]{1,0:T(8,128)(2,1)} fusion(f32[256,768]{1,0:T(8,128)S(1)} %fusion.22, bf16[256,768]{1,0:T(8,128)(2,1)S(1)} %bitcast.25, bf16[768,768]{1,0:T(8,128)(2,1)} %collective-permute-done.3, bf16[256,768]{1,0:T(8,128)(2,1)S(1)} %collective-permute-done.4), kind=kOutput, calls=%fused_computation.5 | convolution fusion | flops 302776320 | bytes 3145728 | tf_op jit(solution)/shard_map/dot_general | solution.py:73
  68.7 10.0 %all-to-all-start.1 = ((bf16[8,32,768]{2,1,0:T(8,128)(2,1)}), bf16[8,32,768]{2,1,0:T(8,128)(2,1)S(1)}, u32[]{:S(2)}, u32[]{:S(2)}) async-start(bf16[8,32,768]{2,1,0:T(8,128)(2,1)} %bitcast.7), calls=%async_computation.1 | async-start | bytes 786432 | tf_op jit(solution)/shard_map/all_to_all | solution.py:84
  78.7 2.1 %shard_map.68 = bf16[512,768]{1,0:T(8,128)(2,1)} custom-call(s32[16]{0:T(128)} %and_select_fusion.refs_0_, bf16[256,768]{1,0:T(8,128)(2,1)} %copy-done.2, bf16[256,768]{1,0:T(8,128)(2,1)} %collective-permute-done.6.refs_2_), custom_call_target="tpu_custom_call" | custom-call | bytes 1 | tf_op jit(solution)/shard_map/pallas_call | solution.py:38
  80.8 3.0 %multiply_convert_fusion = bf16[768,768]{1,0:T(8,128)(2,1)} fusion(bf16[512,768]{1,0:T(8,128)(2,1)} %shard_map.68, bf16[512,768]{1,0:T(8,128)(2,1)S(1)} %bitcast.29), kind=kOutput, calls=%fused_computation.1 | convolution fusion | flops 605159424 | bytes 2752512 | tf_op jit(solution)/shard_map/dot_general | solution.py:92
  83.8 1.9 %collective-permute-start.7 = (bf16[768,768]{1,0:T(8,128)(2,1)}, bf16[768,768]{1,0:T(8,128)(2,1)}, u32[]{:S(2)}, u32[]{:S(2)}) collective-permute-start(bf16[768,768]{1,0:T(8,128)(2,1)} %multiply_convert_fusion), channel_id=1, source_target_pairs={{0,1},{1,0},{2,3},{3,2},{4,5},{5,4},{6,7},{7,6},{8,9},{9,8},{10,11... | collective-permute-start | bytes 3538952 | tf_op jit(solution)/shard_map/ppermute | solution.py:93
  86.6 14.2 %all-to-all-done.1 = bf16[8,32,768]{2,1,0:T(8,128)(2,1)S(1)} async-done(((bf16[8,32,768]{2,1,0:T(8,128)(2,1)}), bf16[8,32,768]{2,1,0:T(8,128)(2,1)S(1)}, u32[]{:S(2)}, u32[]{:S(2)}) %all-to-all-start.1) | async-done | bytes 393248 | tf_op jit(solution)/shard_map/all_to_all | solution.py:84
  101.5 2.6 %add_convert_fusion = bf16[768,768]{1,0:T(8,128)(2,1)} fusion(bf16[768,768]{1,0:T(8,128)(2,1)} %collective-permute-done.7, f32[768,768]{1,0:T(8,128)S(1)} %fusion.24), kind=kLoop, calls=%fused_computation | loop fusion | flops 2359296 | bytes 4718592 | tf_op jit(solution)/shard_map/convert_element_type | solution.py:95
  (27 shorter events, 3.2 us)
Async XLA Ops:
  1.6 3.1 %collective-permute-start = (bf16[32,768]{1,0:T(8,128)(2,1)S(1)}, bf16[32,768]{1,0:T(8,128)(2,1)S(1)}, u32[]{:S(2)}, u32[]{:S(2)}) collective-permute-start(bf16[32,768]{1,0:T(8,128)(2,1)S(1)} %get-tuple-element.19), channel_id=1, source_target_pairs={{0,1},{1,0},{2,3},{3,2},{4,5},{5,4},{6,7},{7,6},{8,9},{9,8},{10,11... | collective-permute-start | bytes 147464 | tf_op jit(solution)/shard_map/ppermute | solution.py:56
  6.1 9.5 %copy-start.1 = (bf16[768,768]{1,0:T(8,128)(2,1)S(1)}, bf16[768,768]{1,0:T(8,128)(2,1)}, u32[]{:S(2)}) copy-start(bf16[768,768]{1,0:T(8,128)(2,1)} %param.8) | copy-start | bytes 3538948
  6.1 11.5 %copy-start.4 = (bf16[32,768]{1,0:T(8,128)(2,1)S(1)}, bf16[32,768]{1,0:T(8,128)(2,1)}, u32[]{:S(2)}) copy-start(bf16[32,768]{1,0:T(8,128)(2,1)} %param.5) | copy-start | bytes 147460
  6.1 35.7 %copy-start.5 = (s32[16]{0:T(128)S(1)}, s32[16]{0:T(128)}, u32[]{:S(2)}) copy-start(s32[16]{0:T(128)} %constant.61.clone) | copy-start | bytes 196
  6.1 39.9 %all-to-all-start = ((bf16[16,2,32,768]{3,2,1,0:T(8,128)(2,1)}), bf16[16,2,32,768]{3,2,1,0:T(8,128)(2,1)S(1)}, u32[]{:S(2)}, u32[]{:S(2)}) async-start(bf16[16,2,32,768]{3,2,1,0:T(8,128)(2,1)} %broadcast_in_dim.2), calls=%async_computation | async-start | bytes 3145728 | tf_op jit(solution)/shard_map/all_to_all | solution.py:60
  15.7 37.3 %collective-permute-start.3 = (bf16[768,768]{1,0:T(8,128)(2,1)S(1)}, bf16[768,768]{1,0:T(8,128)(2,1)}, u32[]{:S(2)}, u32[]{:S(2)}) collective-permute-start(bf16[768,768]{1,0:T(8,128)(2,1)S(1)} %copy-done.1), channel_id=1, source_target_pairs={{0,1},{1,0},{2,3},{3,2},{4,5},{5,4},{6,7},{7,6},{8,9},{9,8},{10,11... | collective-permute-start | bytes 3538952 | tf_op jit(solution)/shard_map/ppermute | solution.py:61
  17.6 16.5 %collective-permute-start.1 = (bf16[32,768]{1,0:T(8,128)(2,1)S(1)}, bf16[32,768]{1,0:T(8,128)(2,1)S(1)}, u32[]{:S(2)}, u32[]{:S(2)}) collective-permute-start(bf16[32,768]{1,0:T(8,128)(2,1)S(1)} %copy-done.4), channel_id=1, source_target_pairs={{0,16},{1,17},{2,18},{3,19},{4,20},{5,21},{6,22},{7,23},{8,24},{9,... | collective-permute-start | bytes 147464 | tf_op jit(solution)/shard_map/ppermute | solution.py:25
  34.1 11.9 %collective-permute-start.2 = (bf16[64,768]{1,0:T(8,128)(2,1)S(1)}, bf16[64,768]{1,0:T(8,128)(2,1)S(1)}, u32[]{:S(2)}, u32[]{:S(2)}) collective-permute-start(bf16[64,768]{1,0:T(8,128)(2,1)S(1)} %pad_maximum_fusion.2), channel_id=1, source_target_pairs={{0,8},{1,25},{2,10},{3,27},{4,12},{5,29},{6,14},{7,31},{8,16},{9,1... | collective-permute-start | bytes 294920 | tf_op jit(solution)/shard_map/ppermute | solution.py:25
  46.0 14.6 %collective-permute-start.5 = (bf16[128,768]{1,0:T(8,128)(2,1)S(1)}, bf16[128,768]{1,0:T(8,128)(2,1)S(1)}, u32[]{:S(2)}, u32[]{:S(2)}) collective-permute-start(bf16[128,768]{1,0:T(8,128)(2,1)S(1)} %pad_maximum_fusion), channel_id=1, source_target_pairs={{0,4},{1,29},{2,6},{3,31},{4,8},{5,1},{6,10},{7,3},{8,12},{9,5},{1... | collective-permute-start | bytes 589832 | tf_op jit(solution)/shard_map/ppermute | solution.py:25
  55.2 10.9 %collective-permute-start.4 = (bf16[256,768]{1,0:T(8,128)(2,1)S(1)}, bf16[256,768]{1,0:T(8,128)(2,1)S(1)}, u32[]{:S(2)}, u32[]{:S(2)}) collective-permute-start(bf16[256,768]{1,0:T(8,128)(2,1)S(1)} %fusion.2), channel_id=1, source_target_pairs={{0,2},{1,31},{2,4},{3,1},{4,6},{5,3},{6,8},{7,5},{8,10},{9,7},{10,... | collective-permute-start | bytes 1179656 | tf_op jit(solution)/shard_map/ppermute | solution.py:25
  60.7 2.9 %copy-start.2 = (bf16[256,768]{1,0:T(8,128)(2,1)}, bf16[256,768]{1,0:T(8,128)(2,1)S(1)}, u32[]{:S(2)}) copy-start(bf16[256,768]{1,0:T(8,128)(2,1)S(1)} %constant_dynamic-update-slice_fusion.refs_1_) | copy-start | bytes 1179652
  60.7 18.0 %collective-permute-start.6 = (bf16[256,768]{1,0:T(8,128)(2,1)S(1)}, bf16[256,768]{1,0:T(8,128)(2,1)}, u32[]{:S(2)}, u32[]{:S(2)}) collective-permute-start(bf16[256,768]{1,0:T(8,128)(2,1)S(1)} %constant_dynamic-update-slice_fusion.refs_1_), channel_id=1, source_target_pairs={{0,2},{1,31},{2,4},{3,1},{4,6},{5,3},{6,8},{7,5},{8,10},{9,7},{10,... | collective-permute-start | bytes 1179656 | tf_op jit(solution)/shard_map/ppermute | solution.py:25
  68.7 12.1 %copy-start.3 = (bf16[16,1,32,768]{3,2,1,0:T(8,128)(2,1)S(1)}, bf16[16,1,32,768]{3,2,1,0:T(8,128)(2,1)}, u32[]{:S(2)}) copy-start(bf16[16,1,32,768]{3,2,1,0:T(8,128)(2,1)} %get-tuple-element.13) | copy-start | bytes 2359300
  68.7 32.1 %all-to-all-start.1 = ((bf16[8,32,768]{2,1,0:T(8,128)(2,1)}), bf16[8,32,768]{2,1,0:T(8,128)(2,1)S(1)}, u32[]{:S(2)}, u32[]{:S(2)}) async-start(bf16[8,32,768]{2,1,0:T(8,128)(2,1)} %bitcast.7), calls=%async_computation.1 | async-start | bytes 786432 | tf_op jit(solution)/shard_map/all_to_all | solution.py:84
  80.8 5.0 %copy-start = (bf16[512,768]{1,0:T(8,128)(2,1)S(1)}, bf16[512,768]{1,0:T(8,128)(2,1)}, u32[]{:S(2)}) copy-start(bf16[512,768]{1,0:T(8,128)(2,1)} %shard_map.68) | copy-start | bytes 2359300
  83.8 17.7 %collective-permute-start.7 = (bf16[768,768]{1,0:T(8,128)(2,1)}, bf16[768,768]{1,0:T(8,128)(2,1)}, u32[]{:S(2)}, u32[]{:S(2)}) collective-permute-start(bf16[768,768]{1,0:T(8,128)(2,1)} %multiply_convert_fusion), channel_id=1, source_target_pairs={{0,1},{1,0},{2,3},{3,2},{4,5},{5,4},{6,7},{7,6},{8,9},{9,8},{10,11... | collective-permute-start | bytes 3538952 | tf_op jit(solution)/shard_map/ppermute | solution.py:93

commit v3 on v1

v3 whole, which is shorter than its diff:
```python
import jax
import jax.numpy as jnp
from jax import lax
from jax.experimental import pallas as pl
from jax.experimental.pallas import tpu as pltpu
from jax.sharding import Mesh, PartitionSpec as P

DEPTH = 16
SWAP = [(0, 1), (1, 0)]
QUARTERS = [list(range(r, DEPTH, 4)) for r in range(4)]
PARITIES = [list(range(0, DEPTH, 2)), list(range(1, DEPTH, 2))]
WHOLE = pl.BlockSpec(memory_space=pltpu.VMEM)


def activation_grad(out_grad, preact):
    value = preact.astype(jnp.float32)
    cdf = 0.5 * (1.0 + jax.scipy.special.erf(value * 0.7071067811865476))
    pdf = jnp.exp(-0.5 * value * value) * 0.3989422804014327
    return (out_grad.astype(jnp.float32) * (cdf + value * pdf)).astype(jnp.bfloat16)


def after(x, y):
    return lax.optimization_barrier((x, y))[0]


def hop(x, step):
    pairs = []
    for z in range(DEPTH):
        pairs.append((2 * z, 2 * ((z + step) % DEPTH)))
        pairs.append((2 * z + 1, 2 * ((z - step) % DEPTH) + 1))
    return lax.ppermute(x, ("z", "core"), pairs)


def call(kernel, out, *arrays, in_specs=None, out_specs=WHOLE, scratch_shapes=(), flops=1 << 20):
    return pl.pallas_call(
        kernel,
        out_shape=out,
        in_specs=in_specs or [WHOLE] * len(arrays),
        out_specs=out_specs,
        scratch_shapes=scratch_shapes,
        compiler_params=pltpu.CompilerParams(vmem_limit_bytes=32 << 20),
        cost_estimate=pl.CostEstimate(flops=flops, bytes_accessed=1 << 20, transcendentals=0),
    )(*arrays)


def tokens(act, which):
    part = act[:, pl.ds(which, 1)]
    return part.reshape(-1, part.shape[-1])


def tokens_of(act, first, cols):
    parts = [tokens(act, lax.rem(first + k, 4))[:, cols] for k in (0, 2)]
    return jnp.concatenate(parts, axis=0)


def dot(a, b, left, right):
    return lax.dot_general(a, b, (((left,), (right,)), ((), ())), preferred_element_type=jnp.float32)


def terms_kernel(parity, act, weight, weight_other, out):
    part = tokens(act, parity[0])
    width = weight.shape[1]
    total = dot(part[:, :width], weight[...], 1, 1) + dot(part[:, width:], weight_other[...], 1, 1)
    out[...] = total.astype(out.dtype)


def sum_kernel(parts, out):
    out[...] = jnp.sum(parts[...].astype(jnp.float32), axis=0).astype(out.dtype)


def for_other_kernel(scale, quarters, act, near, far, out):
    cols = slice(out.shape[1], None)
    total = dot(near[...], tokens_of(act, quarters[0], cols), 0, 0)
    total = total + dot(far[...], tokens_of(act, quarters[1], cols), 0, 0)
    out[...] = (total * scale).astype(out.dtype)


def own_kernel(scale, quarters, act, near, far, got, out):
    cols = slice(None, out.shape[1])
    total = dot(near[...], tokens_of(act, quarters[0], cols), 0, 0)
    total = total + dot(far[...], tokens_of(act, quarters[1], cols), 0, 0)
    out[...] = (total * scale + got[...].astype(jnp.float32)).astype(out.dtype)


def on_device(inputs, out_grad, preact, weight):
    core, z = lax.axis_index("core"), lax.axis_index("z")
    rows, width = inputs.shape[0], weight.shape[1]
    scale = (2 * DEPTH * rows) ** (-0.5)

    def act_of(which, grad):
        part = [lax.dynamic_slice(a, (which * rows, 0), (rows, width)) for a in (grad, preact)]
        return activation_grad(*part)

    leaving = lax.optimization_barrier(act_of(1 - core, out_grad))
    other = lax.ppermute(leaving, "core", SWAP)
    pair = jnp.concatenate([act_of(core, after(out_grad, leaving)), other], axis=1)
    copies = lax.optimization_barrier(jnp.broadcast_to(pair[None], (DEPTH,) + pair.shape))
    arrived = lax.all_to_all(copies, ("y", "x"), 0, 0, tiled=True)
    weight_other = lax.ppermute(after(weight, copies), "core", SWAP)
    quarter = lax.all_gather(after(inputs, copies), "z", axis=0, axis_index_groups=QUARTERS, tiled=True)
    input_near = jnp.concatenate([quarter, hop(after(quarter, weight_other), 2)], axis=0)
    arrived = after(arrived, quarter)

    act = arrived.reshape(DEPTH // 2, 2, rows, 2 * width)
    near = z % 2
    half = (DEPTH // 2 * rows, inputs.shape[1])
    square = jax.ShapeDtypeStruct(weight.shape, jnp.bfloat16)
    flops = 4 * half[0] * half[1] * width
    scalars = pl.BlockSpec(memory_space=pltpu.SMEM)
    def products(parity, dtype):
        return call(
            terms_kernel,
            jax.ShapeDtypeStruct(half, dtype),
            parity.reshape(1), act, weight, weight_other,
            in_specs=[scalars] + [WHOLE] * 3,
            flops=flops,
        )

    far = products(1 - near, jnp.bfloat16)
    below = hop(far, 1)
    total = products(near, jnp.float32)
    input_far = hop(after(input_near, far), 1)
    sent = (total + below.astype(jnp.float32)).astype(jnp.bfloat16).reshape(DEPTH // 2, rows, -1)
    parts = lax.all_to_all(sent, "z", 0, 0, axis_index_groups=PARITIES, tiled=True)
    input_grad = call(sum_kernel, jax.ShapeDtypeStruct(inputs.shape, jnp.bfloat16), parts)

    act = arrived.reshape(4, 4, rows, 2 * width)
    quarters = jnp.stack([z, z + 3 + 2 * core]) % 4
    held = (quarters, act, input_near)
    for_other = call(
        lambda *refs: for_other_kernel(scale, *refs),
        square, *held, after(input_far, sent),
        in_specs=[scalars] + [WHOLE] * 3,
        flops=2 * flops,
    )
    got = lax.ppermute(for_other, "core", SWAP)
    weight_grad = call(
        lambda *refs: own_kernel(scale, *refs),
        square, *held, input_far, got,
        in_specs=[scalars] + [WHOLE] * 4,
        flops=2 * flops,
    )
    return input_grad, weight_grad


def solution(mesh):
    fine = Mesh(mesh.devices.reshape(4, 4, DEPTH, 2), ("y", "x", "z", "core"))
    across, along = ("y", "x"), ("z", "core")
    return jax.shard_map(
        on_device,
        mesh=fine,
        in_specs=(P(along, across), P(across, along), P(across, along), P(across, along)),
        out_specs=(P(along, across), P(across, along)),
        check_vma=False,
    )
```

time: 144 us -> 91.5 us (0.64)
  the two profiles are of different devices: /device:TPU:47 before, /device:TPU:8 now
where the time goes in v3:
time: 91.5 us; the launch traced here: 90.9 us
  starting transfers between devices  31.2 us (34%)
  blocking collectives  25.3 us (28%)
  waiting for transfers between devices  21.3 us (23%)
  Pallas kernels  5.99 us (7%)
  local copies, waits for them, and re-layouts  3.64 us (4%)
  other arithmetic  2.68 us (3%)
    all_gather x1, blocking collectives, on_device(): lax.all_gather(after(inputs, copies), 'z', axis=0, axis_index_groups=QUAR...  25.3 us
    all_to_all x1, waiting for transfers between devices, on_device(): lax.all_to_all(sent, 'z', 0, 0, axis_index_groups=PARITIES, tiled=True)  14.2 us
    all_to_all x1, starting transfers between devices, on_device(): arrived = lax.all_to_all(copies, ('y', 'x'), 0, 0, tiled=True)  9.47 us
    ppermute x3, starting transfers between devices, hop(): return lax.ppermute(x, ('z', 'core'), pairs)  9.34 us
    all_to_all x1, starting transfers between devices, on_device(): lax.all_to_all(sent, 'z', 0, 0, axis_index_groups=PARITIES, tiled=True)  6.65 us
    pallas_call x5, Pallas kernels, call(): pl.pallas_call(kernel, out_shape=out, in_specs=in_specs or [WHOLE] * len(...  5.99 us
    ppermute x3, waiting for transfers between devices, hop(): return lax.ppermute(x, ('z', 'core'), pairs)  3.95 us
    ppermute x1, waiting for transfers between devices, on_device(): got = lax.ppermute(for_other, 'core', SWAP)  2.81 us
  transfers between devices with their start and end apart: 8, of which 5 were waited for; matrix products, arithmetic and copies ran while one was open for 2% of the time, Pallas kernels for 6%

profile of v3, /device:TPU:8, one launch (start us, length us, event | category | flops | bytes accessed | tf_op | source)
XLA Modules:
  0.0 90.9 jit_solution(676977731772373604)
XLA Ops:
  0.6 0.9 fusion.15
  1.5 1.9 %collective-permute-start = (bf16[32,768]{1,0:T(8,128)(2,1)S(1)}, bf16[32,768]{1,0:T(8,128)(2,1)S(1)}, u32[]{:S(2)}, u32[]{:S(2)}) collective-permute-start(bf16[32,768]{1,0:T(8,128)(2,1)S(1)} %fusion.15), channel_id=1, source_target_pairs={{0,1},{1,0},{2,3},{3,2},{4,5},{5,4},{6,7},{7,6},{8,9},{9,8},{10,11... | collective-permute-start | bytes 147464 | tf_op jit(solution)/shard_map/ppermute | solution.py:95
  3.5 0.9 fusion.14
  4.7 1.3 %broadcast_in_dim.2 = bf16[16,32,1536]{2,1,0:T(8,128)(2,1)} broadcast(bf16[32,1536]{1,0:T(8,128)(2,1)S(1)} %pad_maximum_fusion), dimensions={1,2} | broadcast | bytes 1671168 | tf_op jit(solution)/shard_map/broadcast_in_dim | solution.py:97
  6.0 9.5 %all-to-all-start = ((bf16[16,32,1536]{2,1,0:T(8,128)(2,1)}), bf16[16,32,1536]{2,1,0:T(8,128)(2,1)S(1)}, u32[]{:S(2)}, u32[]{:S(2)}) async-start(bf16[16,32,1536]{2,1,0:T(8,128)(2,1)} %broadcast_in_dim.2), calls=%async_computation | async-start | bytes 3145728 | tf_op jit(solution)/shard_map/all_to_all | solution.py:98
  15.5 1.9 %collective-permute-start.1 = (bf16[768,768]{1,0:T(8,128)(2,1)S(1)}, bf16[768,768]{1,0:T(8,128)(2,1)S(1)}, u32[]{:S(2)}, u32[]{:S(2)}) collective-permute-start(bf16[768,768]{1,0:T(8,128)(2,1)S(1)} %copy-done), channel_id=1, source_target_pairs={{0,1},{1,0},{2,3},{3,2},{4,5},{5,4},{6,7},{7,6},{8,9},{9,8},{10,11... | collective-permute-start | bytes 3538952 | tf_op jit(solution)/shard_map/ppermute | solution.py:99
  17.4 25.3 %all_gather.3 = bf16[128,768]{1,0:T(8,128)(2,1)S(1)} all-gather(bf16[32,768]{1,0:T(8,128)(2,1)S(1)} %copy-done.4), channel_id=1, replica_groups={{0,8,16,24},{2,10,18,26},{4,12,20,28},{6,14,22,30},{1,9,17,25},{3,11,19..., dimensions={0}, use_global_device_ids=true | all-gather | bytes 245760 | tf_op jit(solution)/shard_map/all_gather | solution.py:100
  42.7 1.0 %copy-done.1 = bf16[768,768]{1,0:T(8,128)(2,1)} copy-done((bf16[768,768]{1,0:T(8,128)(2,1)}, bf16[768,768]{1,0:T(8,128)(2,1)S(1)}, u32[]{:S(2)}) %copy-start.1) | copy-done | bytes 1179672
  43.7 3.4 %collective-permute-start.3 = (bf16[128,768]{1,0:T(8,128)(2,1)S(1)}, bf16[128,768]{1,0:T(8,128)(2,1)S(1)}, u32[]{:S(2)}, u32[]{:S(2)}) collective-permute-start(bf16[128,768]{1,0:T(8,128)(2,1)S(1)} %all_gather.3), channel_id=1, source_target_pairs={{0,4},{1,29},{2,6},{3,31},{4,8},{5,1},{6,10},{7,3},{8,12},{9,5},{1... | collective-permute-start | bytes 589832 | tf_op jit(solution)/shard_map/ppermute | solution.py:31
  47.2 1.3 %copy-done.2 = bf16[768,768]{1,0:T(8,128)(2,1)S(1)} copy-done((bf16[768,768]{1,0:T(8,128)(2,1)S(1)}, bf16[768,768]{1,0:T(8,128)(2,1)}, u32[]{:S(2)}) %copy-start.2) | copy-done | bytes 1179672
  48.4 0.8 shard_map.60
  49.2 2.9 %collective-permute-start.2 = (bf16[256,768]{1,0:T(8,128)(2,1)S(1)}, bf16[256,768]{1,0:T(8,128)(2,1)S(1)}, u32[]{:S(2)}, u32[]{:S(2)}) collective-permute-start(bf16[256,768]{1,0:T(8,128)(2,1)S(1)} %shard_map.60), channel_id=1, source_target_pairs={{0,2},{1,31},{2,4},{3,1},{4,6},{5,3},{6,8},{7,5},{8,10},{9,7},{10,... | collective-permute-start | bytes 1179656 | tf_op jit(solution)/shard_map/ppermute | solution.py:31
  52.2 3.2 %collective-permute-done.3 = bf16[128,768]{1,0:T(8,128)(2,1)S(1)} collective-permute-done((bf16[128,768]{1,0:T(8,128)(2,1)S(1)}, bf16[128,768]{1,0:T(8,128)(2,1)S(1)}, u32[]{:S(2)}, u32[]{:S(2)}) %collective-permute-start.3) | collective-permute-done | bytes 196640 | tf_op jit(solution)/shard_map/ppermute | solution.py:31
  55.3 3.1 %collective-permute-start.4 = (bf16[256,768]{1,0:T(8,128)(2,1)S(1)}, bf16[256,768]{1,0:T(8,128)(2,1)S(1)}, u32[]{:S(2)}, u32[]{:S(2)}) collective-permute-start(bf16[256,768]{1,0:T(8,128)(2,1)S(1)} %constant_dynamic-update-slice_fusion.refs_2_), channel_id=1, source_target_pairs={{0,2},{1,31},{2,4},{3,1},{4,6},{5,3},{6,8},{7,5},{8,10},{9,7},{10,... | collective-permute-start | bytes 1179656 | tf_op jit(solution)/shard_map/ppermute | solution.py:31
  58.5 0.8 shard_map.59
  59.3 0.8 collective-permute-done.2
  60.1 0.8 add_convert_fusion
  60.9 6.6 %all-to-all-start.1 = ((bf16[8,32,768]{2,1,0:T(8,128)(2,1)}), bf16[8,32,768]{2,1,0:T(8,128)(2,1)S(1)}, u32[]{:S(2)}, u32[]{:S(2)}) async-start(bf16[8,32,768]{2,1,0:T(8,128)(2,1)} %bitcast.3), calls=%async_computation.1 | async-start | bytes 786432 | tf_op jit(solution)/shard_map/all_to_all | solution.py:124
  67.6 1.3 %shard_map.62 = bf16[768,768]{1,0:T(8,128)(2,1)S(1)} custom-call(s32[2]{0:T(128)S(1)} %and_select_fusion.refs_0_, bf16[4,4,32,1536]{3,2,1,0:T(8,128)(2,1)S(1)} %bitcast.9, bf16[256,768]{1,0:T(8,128)(2,1)S(1)} %constant_dynamic-update-slice_fusion.refs_2_, bf16[256,768]{1,0:T(8,128)(2,1)S(1)} %collective-permute-done.4.refs_3_), custom_call_target="tpu_custom_call" | custom-call | flops 1207959552 | bytes 1048576 | tf_op jit(solution)/shard_map/pallas_call | solution.py:35
  68.9 1.9 %collective-permute-start.5 = (bf16[768,768]{1,0:T(8,128)(2,1)S(1)}, bf16[768,768]{1,0:T(8,128)(2,1)S(1)}, u32[]{:S(2)}, u32[]{:S(2)}) collective-permute-start(bf16[768,768]{1,0:T(8,128)(2,1)S(1)} %shard_map.62), channel_id=1, source_target_pairs={{0,1},{1,0},{2,3},{3,2},{4,5},{5,4},{6,7},{7,6},{8,9},{9,8},{10,11... | collective-permute-start | bytes 3538952 | tf_op jit(solution)/shard_map/ppermute | solution.py:136
  70.9 2.8 %collective-permute-done.5.refs_4_ = bf16[768,768]{1,0:T(8,128)(2,1)S(1)} collective-permute-done((bf16[768,768]{1,0:T(8,128)(2,1)S(1)}, bf16[768,768]{1,0:T(8,128)(2,1)S(1)}, u32[]{:S(2)}, u32[]{:S(2)}) %collective-permute-start.5) | collective-permute-done | bytes 1179680 | tf_op jit(solution)/shard_map/ppermute | solution.py:136
  73.7 2.4 %shard_map.63 = bf16[768,768]{1,0:T(8,128)(2,1)} custom-call(s32[2]{0:T(128)S(1)} %and_select_fusion.refs_0_, bf16[4,4,32,1536]{3,2,1,0:T(8,128)(2,1)S(1)} %bitcast.10, bf16[256,768]{1,0:T(8,128)(2,1)S(1)} %constant_dynamic-update-slice_fusion.refs_2_, bf16[256,768]{1,0:T(8,128)(2,1)S(1)} %collective-permute-done.4.refs_3_, ...), custom_call_target="tpu_custom_call" | custom-call | flops 1207959552 | bytes 1048576 | tf_op jit(solution)/shard_map/pallas_call | solution.py:35
  76.1 14.2 %all-to-all-done.1.parts = bf16[8,32,768]{2,1,0:T(8,128)(2,1)S(1)} async-done(((bf16[8,32,768]{2,1,0:T(8,128)(2,1)}), bf16[8,32,768]{2,1,0:T(8,128)(2,1)S(1)}, u32[]{:S(2)}, u32[]{:S(2)}) %all-to-all-start.1) | async-done | bytes 393248 | tf_op jit(solution)/shard_map/all_to_all | solution.py:124
  90.2 0.7 shard_map.61
  (16 shorter events, 0.5 us)
Async XLA Ops:
  1.5 3.1 %collective-permute-start = (bf16[32,768]{1,0:T(8,128)(2,1)S(1)}, bf16[32,768]{1,0:T(8,128)(2,1)S(1)}, u32[]{:S(2)}, u32[]{:S(2)}) collective-permute-start(bf16[32,768]{1,0:T(8,128)(2,1)S(1)} %fusion.15), channel_id=1, source_target_pairs={{0,1},{1,0},{2,3},{3,2},{4,5},{5,4},{6,7},{7,6},{8,9},{9,8},{10,11... | collective-permute-start | bytes 147464 | tf_op jit(solution)/shard_map/ppermute | solution.py:95
  6.0 9.5 %copy-start = (bf16[768,768]{1,0:T(8,128)(2,1)S(1)}, bf16[768,768]{1,0:T(8,128)(2,1)}, u32[]{:S(2)}) copy-start(bf16[768,768]{1,0:T(8,128)(2,1)} %weight.3) | copy-start | bytes 3538948
  6.0 11.4 %copy-start.4 = (bf16[32,768]{1,0:T(8,128)(2,1)S(1)}, bf16[32,768]{1,0:T(8,128)(2,1)}, u32[]{:S(2)}) copy-start(bf16[32,768]{1,0:T(8,128)(2,1)} %param.4) | copy-start | bytes 147460
  6.0 41.2 %all-to-all-start = ((bf16[16,32,1536]{2,1,0:T(8,128)(2,1)}), bf16[16,32,1536]{2,1,0:T(8,128)(2,1)S(1)}, u32[]{:S(2)}, u32[]{:S(2)}) async-start(bf16[16,32,1536]{2,1,0:T(8,128)(2,1)} %broadcast_in_dim.2), calls=%async_computation | async-start | bytes 3145728 | tf_op jit(solution)/shard_map/all_to_all | solution.py:98
  15.5 27.3 %collective-permute-start.1 = (bf16[768,768]{1,0:T(8,128)(2,1)S(1)}, bf16[768,768]{1,0:T(8,128)(2,1)S(1)}, u32[]{:S(2)}, u32[]{:S(2)}) collective-permute-start(bf16[768,768]{1,0:T(8,128)(2,1)S(1)} %copy-done), channel_id=1, source_target_pairs={{0,1},{1,0},{2,3},{3,2},{4,5},{5,4},{6,7},{7,6},{8,9},{9,8},{10,11... | collective-permute-start | bytes 3538952 | tf_op jit(solution)/shard_map/ppermute | solution.py:99
  42.7 1.0 %copy-start.1 = (bf16[768,768]{1,0:T(8,128)(2,1)}, bf16[768,768]{1,0:T(8,128)(2,1)S(1)}, u32[]{:S(2)}) copy-start(bf16[768,768]{1,0:T(8,128)(2,1)S(1)} %collective-permute-done.1.weight_other) | copy-start | bytes 3538948
  43.7 11.6 %collective-permute-start.3 = (bf16[128,768]{1,0:T(8,128)(2,1)S(1)}, bf16[128,768]{1,0:T(8,128)(2,1)S(1)}, u32[]{:S(2)}, u32[]{:S(2)}) collective-permute-start(bf16[128,768]{1,0:T(8,128)(2,1)S(1)} %all_gather.3), channel_id=1, source_target_pairs={{0,4},{1,29},{2,6},{3,31},{4,8},{5,1},{6,10},{7,3},{8,12},{9,5},{1... | collective-permute-start | bytes 589832 | tf_op jit(solution)/shard_map/ppermute | solution.py:31
  47.1 1.3 %copy-start.2 = (bf16[768,768]{1,0:T(8,128)(2,1)S(1)}, bf16[768,768]{1,0:T(8,128)(2,1)}, u32[]{:S(2)}) copy-start(bf16[768,768]{1,0:T(8,128)(2,1)} %copy-done.1) | copy-start | bytes 3538948
  48.4 10.1 %copy-start.3 = (bf16[768,768]{1,0:T(8,128)(2,1)S(1)}, bf16[768,768]{1,0:T(8,128)(2,1)}, u32[]{:S(2)}) copy-start(bf16[768,768]{1,0:T(8,128)(2,1)} %copy-done.1) | copy-start | bytes 3538948
  49.2 10.9 %collective-permute-start.2 = (bf16[256,768]{1,0:T(8,128)(2,1)S(1)}, bf16[256,768]{1,0:T(8,128)(2,1)S(1)}, u32[]{:S(2)}, u32[]{:S(2)}) collective-permute-start(bf16[256,768]{1,0:T(8,128)(2,1)S(1)} %shard_map.60), channel_id=1, source_target_pairs={{0,2},{1,31},{2,4},{3,1},{4,6},{5,3},{6,8},{7,5},{8,10},{9,7},{10,... | collective-permute-start | bytes 1179656 | tf_op jit(solution)/shard_map/ppermute | solution.py:31
  55.3 12.2 %collective-permute-start.4 = (bf16[256,768]{1,0:T(8,128)(2,1)S(1)}, bf16[256,768]{1,0:T(8,128)(2,1)S(1)}, u32[]{:S(2)}, u32[]{:S(2)}) collective-permute-start(bf16[256,768]{1,0:T(8,128)(2,1)S(1)} %constant_dynamic-update-slice_fusion.refs_2_), channel_id=1, source_target_pairs={{0,2},{1,31},{2,4},{3,1},{4,6},{5,3},{6,8},{7,5},{8,10},{9,7},{10,... | collective-permute-start | bytes 1179656 | tf_op jit(solution)/shard_map/ppermute | solution.py:31
  60.9 29.3 %all-to-all-start.1 = ((bf16[8,32,768]{2,1,0:T(8,128)(2,1)}), bf16[8,32,768]{2,1,0:T(8,128)(2,1)S(1)}, u32[]{:S(2)}, u32[]{:S(2)}) async-start(bf16[8,32,768]{2,1,0:T(8,128)(2,1)} %bitcast.3), calls=%async_computation.1 | async-start | bytes 786432 | tf_op jit(solution)/shard_map/all_to_all | solution.py:124
  68.9 4.7 %collective-permute-start.5 = (bf16[768,768]{1,0:T(8,128)(2,1)S(1)}, bf16[768,768]{1,0:T(8,128)(2,1)S(1)}, u32[]{:S(2)}, u32[]{:S(2)}) collective-permute-start(bf16[768,768]{1,0:T(8,128)(2,1)S(1)} %shard_map.62), channel_id=1, source_target_pairs={{0,1},{1,0},{2,3},{3,2},{4,5},{5,4},{6,7},{7,6},{8,9},{9,8},{10,11... | collective-permute-start | bytes 3538952 | tf_op jit(solution)/shard_map/ppermute | solution.py:136

commit v4 on v3

--- a/solution.py
+++ b/solution.py
@@ -31,6 +31,10 @@
     return lax.ppermute(x, ("z", "core"), pairs)
 
 
+def shift(x, step):
+    return lax.ppermute(x, "z", [(z, (z + step) % DEPTH) for z in range(DEPTH)])
+
+
 def call(kernel, out, *arrays, in_specs=None, out_specs=WHOLE, scratch_shapes=(), flops=1 << 20):
     return pl.pallas_call(
         kernel,
@@ -53,6 +57,12 @@
     return jnp.concatenate(parts, axis=0)
 
 
+def join_kernel(first, second, out):
+    rows = first.shape[0]
+    out[:rows] = first[...]
+    out[rows:] = second[...]
+
+
 def dot(a, b, left, right):
     return lax.dot_general(a, b, (((left,), (right,)), ((), ())), preferred_element_type=jnp.float32)
 
@@ -64,21 +74,25 @@
     out[...] = total.astype(out.dtype)
 
 
+def add_kernel(total, below, out):
+    out[...] = (total[...] + below[...].astype(jnp.float32)).astype(out.dtype).reshape(out.shape)
+
+
 def sum_kernel(parts, out):
     out[...] = jnp.sum(parts[...].astype(jnp.float32), axis=0).astype(out.dtype)
 
 
-def for_other_kernel(scale, quarters, act, near, far, out):
+def for_other_kernel(scale, z, act, near, far, out):
     cols = slice(out.shape[1], None)
-    total = dot(near[...], tokens_of(act, quarters[0], cols), 0, 0)
-    total = total + dot(far[...], tokens_of(act, quarters[1], cols), 0, 0)
+    total = dot(near[...], tokens_of(act, z[0], cols), 0, 0)
+    total = total + dot(far[...], tokens_of(act, z[0] + 1, cols), 0, 0)
     out[...] = (total * scale).astype(out.dtype)
 
 
-def own_kernel(scale, quarters, act, near, far, got, out):
+def own_kernel(scale, z, act, near, far, got, out):
     cols = slice(None, out.shape[1])
-    total = dot(near[...], tokens_of(act, quarters[0], cols), 0, 0)
-    total = total + dot(far[...], tokens_of(act, quarters[1], cols), 0, 0)
+    total = dot(near[...], tokens_of(act, z[0], cols), 0, 0)
+    total = total + dot(far[...], tokens_of(act, z[0] + 1, cols), 0, 0)
     out[...] = (total * scale + got[...].astype(jnp.float32)).astype(out.dtype)
 
 
@@ -98,12 +112,13 @@
     arrived = lax.all_to_all(copies, ("y", "x"), 0, 0, tiled=True)
     weight_other = lax.ppermute(after(weight, copies), "core", SWAP)
     quarter = lax.all_gather(after(inputs, copies), "z", axis=0, axis_index_groups=QUARTERS, tiled=True)
-    input_near = jnp.concatenate([quarter, hop(after(quarter, weight_other), 2)], axis=0)
+    second = hop(quarter, 2)
     arrived = after(arrived, quarter)
 
     act = arrived.reshape(DEPTH // 2, 2, rows, 2 * width)
     near = z % 2
     half = (DEPTH // 2 * rows, inputs.shape[1])
+    input_near = call(join_kernel, jax.ShapeDtypeStruct(half, inputs.dtype), quarter, second)
     square = jax.ShapeDtypeStruct(weight.shape, jnp.bfloat16)
     flops = 4 * half[0] * half[1] * width
     scalars = pl.BlockSpec(memory_space=pltpu.SMEM)
@@ -119,14 +134,13 @@
     far = products(1 - near, jnp.bfloat16)
     below = hop(far, 1)
     total = products(near, jnp.float32)
-    input_far = hop(after(input_near, far), 1)
-    sent = (total + below.astype(jnp.float32)).astype(jnp.bfloat16).reshape(DEPTH // 2, rows, -1)
+    input_far = shift(after(input_near, far), -1)
+    sent = call(add_kernel, jax.ShapeDtypeStruct((DEPTH // 2, rows, half[1]), jnp.bfloat16), total, below)
     parts = lax.all_to_all(sent, "z", 0, 0, axis_index_groups=PARITIES, tiled=True)
     input_grad = call(sum_kernel, jax.ShapeDtypeStruct(inputs.shape, jnp.bfloat16), parts)
 
     act = arrived.reshape(4, 4, rows, 2 * width)
-    quarters = jnp.stack([z, z + 3 + 2 * core]) % 4
-    held = (quarters, act, input_near)
+    held = (z.reshape(1), act, input_near)
     for_other = call(
         lambda *refs: for_other_kernel(scale, *refs),
         square, *held, after(input_far, sent),

time: 91.5 us -> 91 us (level)
  the two profiles are of different devices: /device:TPU:8 before, /device:TPU:64 now
where the time goes in v4:
time: 91 us; the launch traced here: 90.4 us
  starting transfers between devices  33.4 us (37%)
  blocking collectives  25.5 us (28%)
  waiting for transfers between devices  19.3 us (21%)
  Pallas kernels  8.29 us (9%)
  other arithmetic  1.77 us (2%)
  local copies, waits for them, and re-layouts  1.31 us (1%)
    all_gather x1, blocking collectives, on_device(): lax.all_gather(after(inputs, copies), 'z', axis=0, axis_index_groups=QUAR...  25.5 us
    all_to_all x1, waiting for transfers between devices, on_device(): lax.all_to_all(sent, 'z', 0, 0, axis_index_groups=PARITIES, tiled=True)  15.4 us
    all_to_all x1, starting transfers between devices, on_device(): lax.all_to_all(sent, 'z', 0, 0, axis_index_groups=PARITIES, tiled=True)  9.27 us
    pallas_call x7, Pallas kernels, call(): pl.pallas_call(kernel, out_shape=out, in_specs=in_specs or [WHOLE] * len(...  8.29 us
    all_to_all x1, starting transfers between devices, on_device(): arrived = lax.all_to_all(copies, ('y', 'x'), 0, 0, tiled=True)  7.17 us
    ppermute x2, starting transfers between devices, hop(): return lax.ppermute(x, ('z', 'core'), pairs)  6.24 us
    ppermute x1, starting transfers between devices, shift(): return lax.ppermute(x, 'z', [(z, (z + step) % DEPTH) for z in range(DEPTH)])  4.99 us
    ppermute x1, waiting for transfers between devices, on_device(): got = lax.ppermute(for_other, 'core', SWAP)  2.81 us
  transfers between devices with their start and end apart: 8, of which 4 were waited for; matrix products, arithmetic and copies ran while one was open for 1% of the time, Pallas kernels for 8%

profile of v4, /device:TPU:64, one launch (start us, length us, event | category | flops | bytes accessed | tf_op | source)
XLA Modules:
  0.0 90.4 jit_solution(17276890499403033446)
XLA Ops:
  0.6 0.9 fusion.15
  1.5 1.9 %collective-permute-start = (bf16[32,768]{1,0:T(8,128)(2,1)S(1)}, bf16[32,768]{1,0:T(8,128)(2,1)S(1)}, u32[]{:S(2)}, u32[]{:S(2)}) collective-permute-start(bf16[32,768]{1,0:T(8,128)(2,1)S(1)} %fusion.15), channel_id=1, source_target_pairs={{0,1},{1,0},{2,3},{3,2},{4,5},{5,4},{6,7},{7,6},{8,9},{9,8},{10,11... | collective-permute-start | bytes 147464 | tf_op jit(solution)/shard_map/ppermute | solution.py:109
  3.4 0.9 fusion.14
  4.3 0.3 collective-permute-done
  4.7 1.3 %broadcast_in_dim.2 = bf16[16,32,1536]{2,1,0:T(8,128)(2,1)} broadcast(bf16[32,1536]{1,0:T(8,128)(2,1)S(1)} %pad_maximum_fusion), dimensions={1,2} | broadcast | bytes 1671168 | tf_op jit(solution)/shard_map/broadcast_in_dim | solution.py:111
  6.0 7.2 %all-to-all-start = ((bf16[16,32,1536]{2,1,0:T(8,128)(2,1)}), bf16[16,32,1536]{2,1,0:T(8,128)(2,1)S(1)}, u32[]{:S(2)}, u32[]{:S(2)}) async-start(bf16[16,32,1536]{2,1,0:T(8,128)(2,1)} %broadcast_in_dim.2), calls=%async_computation | async-start | bytes 3145728 | tf_op jit(solution)/shard_map/all_to_all | solution.py:112
  13.1 1.9 %collective-permute-start.1 = (bf16[768,768]{1,0:T(8,128)(2,1)S(1)}, bf16[768,768]{1,0:T(8,128)(2,1)}, u32[]{:S(2)}, u32[]{:S(2)}) collective-permute-start(bf16[768,768]{1,0:T(8,128)(2,1)S(1)} %copy-done), channel_id=1, source_target_pairs={{0,1},{1,0},{2,3},{3,2},{4,5},{5,4},{6,7},{7,6},{8,9},{9,8},{10,11... | collective-permute-start | bytes 3538952 | tf_op jit(solution)/shard_map/ppermute | solution.py:113
  15.1 25.5 %all_gather.3.first = bf16[128,768]{1,0:T(8,128)(2,1)S(1)} all-gather(bf16[32,768]{1,0:T(8,128)(2,1)S(1)} %copy-done.1), channel_id=1, replica_groups={{0,8,16,24},{2,10,18,26},{4,12,20,28},{6,14,22,30},{1,9,17,25},{3,11,19..., dimensions={0}, use_global_device_ids=true | all-gather | bytes 245760 | tf_op jit(solution)/shard_map/all_gather | solution.py:114
  40.6 4.0 %collective-permute-start.3 = (bf16[128,768]{1,0:T(8,128)(2,1)S(1)}, bf16[128,768]{1,0:T(8,128)(2,1)S(1)}, u32[]{:S(2)}, u32[]{:S(2)}) collective-permute-start(bf16[128,768]{1,0:T(8,128)(2,1)S(1)} %all_gather.3.first), channel_id=1, source_target_pairs={{0,4},{1,29},{2,6},{3,31},{4,8},{5,1},{6,10},{7,3},{8,12},{9,5},{1... | collective-permute-start | bytes 589832 | tf_op jit(solution)/shard_map/ppermute | solution.py:31
  44.6 0.0 all-to-all-done
  44.6 0.0 collective-permute-done.1.weight_other
  44.6 2.1 %shard_map.60 = bf16[256,768]{1,0:T(8,128)(2,1)S(1)} custom-call(s32[1]{0:T(128)} %bitcast.2.parity, bf16[8,2,32,1536]{3,2,1,0:T(8,128)(2,1)S(1)} %bitcast.5, bf16[768,768]{1,0:T(8,128)(2,1)S(1)} %copy-done, bf16[768,768]{1,0:T(8,128)(2,1)} %collective-permute-done.1.weight_other), custom_call_target="tpu_custom_call" | custom-call | flops 603979776 | bytes 1048576 | tf_op jit(solution)/shard_map/pallas_call | solution.py:39
  46.7 2.3 %collective-permute-start.2 = (bf16[256,768]{1,0:T(8,128)(2,1)S(1)}, bf16[256,768]{1,0:T(8,128)(2,1)S(1)}, u32[]{:S(2)}, u32[]{:S(2)}) collective-permute-start(bf16[256,768]{1,0:T(8,128)(2,1)S(1)} %shard_map.60), channel_id=1, source_target_pairs={{0,2},{1,31},{2,4},{3,1},{4,6},{5,3},{6,8},{7,5},{8,10},{9,7},{10,... | collective-permute-start | bytes 1179656 | tf_op jit(solution)/shard_map/ppermute | solution.py:31
  48.9 0.8 collective-permute-done.3.second
  49.7 5.0 %collective-permute-start.4 = (bf16[256,768]{1,0:T(8,128)(2,1)S(1)}, bf16[256,768]{1,0:T(8,128)(2,1)S(1)}, u32[]{:S(2)}, u32[]{:S(2)}) collective-permute-start(bf16[256,768]{1,0:T(8,128)(2,1)S(1)} %shard_map.63.refs_2_), channel_id=1, source_target_pairs={{0,30},{2,0},{4,2},{6,4},{8,6},{10,8},{12,10},{14,12},{16,14},{18,... | collective-permute-start | bytes 1179656 | tf_op jit(solution)/shard_map/ppermute | solution.py:35
  54.7 2.1 %shard_map.59.total = f32[256,768]{1,0:T(8,128)S(1)} custom-call(s32[1]{0:T(128)} %bitcast.parity, bf16[8,2,32,1536]{3,2,1,0:T(8,128)(2,1)S(1)} %bitcast.6, bf16[768,768]{1,0:T(8,128)(2,1)S(1)} %copy-done, bf16[768,768]{1,0:T(8,128)(2,1)} %collective-permute-done.1.weight_other), custom_call_target="tpu_custom_call" | custom-call | flops 603979776 | bytes 1048576 | tf_op jit(solution)/shard_map/pallas_call | solution.py:39
  56.8 0.8 shard_map.61
  57.6 9.3 %all-to-all-start.1 = ((bf16[8,32,768]{2,1,0:T(8,128)(2,1)}), bf16[8,32,768]{2,1,0:T(8,128)(2,1)S(1)}, u32[]{:S(2)}, u32[]{:S(2)}) async-start(bf16[8,32,768]{2,1,0:T(8,128)(2,1)} %shard_map.61), calls=%async_computation.1 | async-start | bytes 786432 | tf_op jit(solution)/shard_map/all_to_all | solution.py:139
  66.9 0.8 shard_map.64
  67.7 1.9 %collective-permute-start.5 = (bf16[768,768]{1,0:T(8,128)(2,1)S(1)}, bf16[768,768]{1,0:T(8,128)(2,1)S(1)}, u32[]{:S(2)}, u32[]{:S(2)}) collective-permute-start(bf16[768,768]{1,0:T(8,128)(2,1)S(1)} %shard_map.64), channel_id=1, source_target_pairs={{0,1},{1,0},{2,3},{3,2},{4,5},{5,4},{6,7},{7,6},{8,9},{9,8},{10,11... | collective-permute-start | bytes 3538952 | tf_op jit(solution)/shard_map/ppermute | solution.py:150
  69.7 2.8 %collective-permute-done.5.refs_4_ = bf16[768,768]{1,0:T(8,128)(2,1)S(1)} collective-permute-done((bf16[768,768]{1,0:T(8,128)(2,1)S(1)}, bf16[768,768]{1,0:T(8,128)(2,1)S(1)}, u32[]{:S(2)}, u32[]{:S(2)}) %collective-permute-start.5) | collective-permute-done | bytes 1179680 | tf_op jit(solution)/shard_map/ppermute | solution.py:150
  72.5 1.8 %shard_map.65 = bf16[768,768]{1,0:T(8,128)(2,1)} custom-call(s32[1]{0:T(128)} %bitcast.3.refs_0_, bf16[4,4,32,1536]{3,2,1,0:T(8,128)(2,1)S(1)} %bitcast.8, bf16[256,768]{1,0:T(8,128)(2,1)S(1)} %shard_map.63.refs_2_, bf16[256,768]{1,0:T(8,128)(2,1)S(1)} %collective-permute-done.4.refs_3_, bf16[768,768]{1,0:T(8,128)(2,1)S(1)} %collective-permute-done.5.refs_4_), custom_call_target="tpu_custom_call" | custom-call | flops 1207959552 | bytes 1048576 | tf_op jit(solution)/shard_map/pallas_call | solution.py:39
  74.3 15.4 %all-to-all-done.1.parts = bf16[8,32,768]{2,1,0:T(8,128)(2,1)S(1)} async-done(((bf16[8,32,768]{2,1,0:T(8,128)(2,1)}), bf16[8,32,768]{2,1,0:T(8,128)(2,1)S(1)}, u32[]{:S(2)}, u32[]{:S(2)}) %all-to-all-start.1) | async-done | bytes 393248 | tf_op jit(solution)/shard_map/all_to_all | solution.py:139
  89.7 0.7 shard_map.62
  (8 shorter events, 0.0 us)
Async XLA Ops:
  1.5 3.1 %collective-permute-start = (bf16[32,768]{1,0:T(8,128)(2,1)S(1)}, bf16[32,768]{1,0:T(8,128)(2,1)S(1)}, u32[]{:S(2)}, u32[]{:S(2)}) collective-permute-start(bf16[32,768]{1,0:T(8,128)(2,1)S(1)} %fusion.15), channel_id=1, source_target_pairs={{0,1},{1,0},{2,3},{3,2},{4,5},{5,4},{6,7},{7,6},{8,9},{9,8},{10,11... | collective-permute-start | bytes 147464 | tf_op jit(solution)/shard_map/ppermute | solution.py:109
  6.0 7.2 %copy-start = (bf16[768,768]{1,0:T(8,128)(2,1)S(1)}, bf16[768,768]{1,0:T(8,128)(2,1)}, u32[]{:S(2)}) copy-start(bf16[768,768]{1,0:T(8,128)(2,1)} %weight.3) | copy-start | bytes 3538948
  6.0 9.1 %copy-start.1 = (bf16[32,768]{1,0:T(8,128)(2,1)S(1)}, bf16[32,768]{1,0:T(8,128)(2,1)}, u32[]{:S(2)}) copy-start(bf16[32,768]{1,0:T(8,128)(2,1)} %param.4) | copy-start | bytes 147460
  6.0 38.6 %all-to-all-start = ((bf16[16,32,1536]{2,1,0:T(8,128)(2,1)}), bf16[16,32,1536]{2,1,0:T(8,128)(2,1)S(1)}, u32[]{:S(2)}, u32[]{:S(2)}) async-start(bf16[16,32,1536]{2,1,0:T(8,128)(2,1)} %broadcast_in_dim.2), calls=%async_computation | async-start | bytes 3145728 | tf_op jit(solution)/shard_map/all_to_all | solution.py:112
  13.1 31.4 %collective-permute-start.1 = (bf16[768,768]{1,0:T(8,128)(2,1)S(1)}, bf16[768,768]{1,0:T(8,128)(2,1)}, u32[]{:S(2)}, u32[]{:S(2)}) collective-permute-start(bf16[768,768]{1,0:T(8,128)(2,1)S(1)} %copy-done), channel_id=1, source_target_pairs={{0,1},{1,0},{2,3},{3,2},{4,5},{5,4},{6,7},{7,6},{8,9},{9,8},{10,11... | collective-permute-start | bytes 3538952 | tf_op jit(solution)/shard_map/ppermute | solution.py:113
  40.6 9.1 %collective-permute-start.3 = (bf16[128,768]{1,0:T(8,128)(2,1)S(1)}, bf16[128,768]{1,0:T(8,128)(2,1)S(1)}, u32[]{:S(2)}, u32[]{:S(2)}) collective-permute-start(bf16[128,768]{1,0:T(8,128)(2,1)S(1)} %all_gather.3.first), channel_id=1, source_target_pairs={{0,4},{1,29},{2,6},{3,31},{4,8},{5,1},{6,10},{7,3},{8,12},{9,5},{1... | collective-permute-start | bytes 589832 | tf_op jit(solution)/shard_map/ppermute | solution.py:31
  46.7 10.2 %collective-permute-start.2 = (bf16[256,768]{1,0:T(8,128)(2,1)S(1)}, bf16[256,768]{1,0:T(8,128)(2,1)S(1)}, u32[]{:S(2)}, u32[]{:S(2)}) collective-permute-start(bf16[256,768]{1,0:T(8,128)(2,1)S(1)} %shard_map.60), channel_id=1, source_target_pairs={{0,2},{1,31},{2,4},{3,1},{4,6},{5,3},{6,8},{7,5},{8,10},{9,7},{10,... | collective-permute-start | bytes 1179656 | tf_op jit(solution)/shard_map/ppermute | solution.py:31
  49.7 17.2 %collective-permute-start.4 = (bf16[256,768]{1,0:T(8,128)(2,1)S(1)}, bf16[256,768]{1,0:T(8,128)(2,1)S(1)}, u32[]{:S(2)}, u32[]{:S(2)}) collective-permute-start(bf16[256,768]{1,0:T(8,128)(2,1)S(1)} %shard_map.63.refs_2_), channel_id=1, source_target_pairs={{0,30},{2,0},{4,2},{6,4},{8,6},{10,8},{12,10},{14,12},{16,14},{18,... | collective-permute-start | bytes 1179656 | tf_op jit(solution)/shard_map/ppermute | solution.py:35
  57.6 32.0 %all-to-all-start.1 = ((bf16[8,32,768]{2,1,0:T(8,128)(2,1)}), bf16[8,32,768]{2,1,0:T(8,128)(2,1)S(1)}, u32[]{:S(2)}, u32[]{:S(2)}) async-start(bf16[8,32,768]{2,1,0:T(8,128)(2,1)} %shard_map.61), calls=%async_computation.1 | async-start | bytes 786432 | tf_op jit(solution)/shard_map/all_to_all | solution.py:139
  67.7 4.7 %collective-permute-start.5 = (bf16[768,768]{1,0:T(8,128)(2,1)S(1)}, bf16[768,768]{1,0:T(8,128)(2,1)S(1)}, u32[]{:S(2)}, u32[]{:S(2)}) collective-permute-start(bf16[768,768]{1,0:T(8,128)(2,1)S(1)} %shard_map.64), channel_id=1, source_target_pairs={{0,1},{1,0},{2,3},{3,2},{4,5},{5,4},{6,7},{7,6},{8,9},{9,8},{10,11... | collective-permute-start | bytes 3538952 | tf_op jit(solution)/shard_map/ppermute | solution.py:150

commit v5 on v4

--- a/solution.py
+++ b/solution.py
@@ -8,7 +8,8 @@
 DEPTH = 16
 SWAP = [(0, 1), (1, 0)]
 QUARTERS = [list(range(r, DEPTH, 4)) for r in range(4)]
-PARITIES = [list(range(0, DEPTH, 2)), list(range(1, DEPTH, 2))]
+ORDER = (0, 4, 2, 6, 1, 5, 3, 7)
+PARITIES = [[2 * j + p for j in ORDER] for p in (0, 1)]
 WHOLE = pl.BlockSpec(memory_space=pltpu.VMEM)
 
 
@@ -75,7 +76,9 @@
 
 
 def add_kernel(total, below, out):
-    out[...] = (total[...] + below[...].astype(jnp.float32)).astype(out.dtype).reshape(out.shape)
+    summed = (total[...] + below[...].astype(jnp.float32)).astype(out.dtype).reshape(out.shape)
+    for k, j in enumerate(ORDER):
+        out[k] = summed[j]
 
 
 def sum_kernel(parts, out):

time: 91 us -> 87 us (0.956)
  the two profiles are of different devices: /device:TPU:64 before, /device:TPU:129 now
where the time goes in v5:
time: 87 us; the launch traced here: 86.3 us
  starting transfers between devices  40.7 us (47%)
  blocking collectives  18.8 us (22%)
  waiting for transfers between devices  14.6 us (17%)
  Pallas kernels  8.28 us (10%)
  other arithmetic  1.77 us (2%)
  local copies, waits for them, and re-layouts  1.31 us (2%)
    all_gather x1, blocking collectives, on_device(): lax.all_gather(after(inputs, copies), 'z', axis=0, axis_index_groups=QUAR...  18.8 us
    all_to_all x1, waiting for transfers between devices, on_device(): lax.all_to_all(sent, 'z', 0, 0, axis_index_groups=PARITIES, tiled=True)  12 us
    all_to_all x1, starting transfers between devices, on_device(): lax.all_to_all(sent, 'z', 0, 0, axis_index_groups=PARITIES, tiled=True)  10.7 us
    pallas_call x7, Pallas kernels, call(): pl.pallas_call(kernel, out_shape=out, in_specs=in_specs or [WHOLE] * len(...  8.28 us
    ppermute x2, starting transfers between devices, hop(): return lax.ppermute(x, ('z', 'core'), pairs)  7.11 us
    all_to_all x1, starting transfers between devices, on_device(): arrived = lax.all_to_all(copies, ('y', 'x'), 0, 0, tiled=True)  6.89 us
    ppermute x1, starting transfers between devices, on_device(): got = lax.ppermute(for_other, 'core', SWAP)  5.94 us
    ppermute x1, starting transfers between devices, shift(): return lax.ppermute(x, 'z', [(z, (z + step) % DEPTH) for z in range(DEPTH)])  5.05 us
  transfers between devices with their start and end apart: 8, of which 3 were waited for; matrix products, arithmetic and copies ran while one was open for 1% of the time, Pallas kernels for 9%

profile of v5, /device:TPU:129, one launch (start us, length us, event | category | flops | bytes accessed | tf_op | source)
XLA Modules:
  0.0 86.3 jit_solution(11362281667047818554)
XLA Ops:
  0.6 0.9 %fusion.15 = bf16[32,768]{1,0:T(8,128)(2,1)S(1)} fusion(bf16[64,768]{1,0:T(8,128)(2,1)} %param.6, s32[]{:T(128)S(6)} %select_n.16, bf16[64,768]{1,0:T(8,128)(2,1)} %param.5), kind=kLoop, calls=%fused_computation.24 | loop fusion | flops 294912 | bytes 147460 | tf_op jit(solution)/shard_map/convert_element_type | solution.py:20
  1.5 2.6 %collective-permute-start = (bf16[32,768]{1,0:T(8,128)(2,1)S(1)}, bf16[32,768]{1,0:T(8,128)(2,1)S(1)}, u32[]{:S(2)}, u32[]{:S(2)}) collective-permute-start(bf16[32,768]{1,0:T(8,128)(2,1)S(1)} %fusion.15), channel_id=1, source_target_pairs={{0,1},{1,0},{2,3},{3,2},{4,5},{5,4},{6,7},{7,6},{8,9},{9,8},{10,11... | collective-permute-start | bytes 147464 | tf_op jit(solution)/shard_map/ppermute | solution.py:112
  4.1 0.9 %fusion.14 = bf16[32,768]{1,0:T(8,128)(2,1)S(1)} fusion(bf16[64,768]{1,0:T(8,128)(2,1)} %param.6, s32[]{:T(128)S(6)} %select_n.17, bf16[64,768]{1,0:T(8,128)(2,1)} %param.5), kind=kLoop, calls=%fused_computation.23 | loop fusion | flops 294912 | bytes 147460 | tf_op jit(solution)/shard_map/convert_element_type | solution.py:20
  5.0 1.3 %broadcast_in_dim.2 = bf16[16,32,1536]{2,1,0:T(8,128)(2,1)} broadcast(bf16[32,1536]{1,0:T(8,128)(2,1)S(1)} %pad_maximum_fusion), dimensions={1,2} | broadcast | bytes 1671168 | tf_op jit(solution)/shard_map/broadcast_in_dim | solution.py:114
  6.3 6.9 %all-to-all-start = ((bf16[16,32,1536]{2,1,0:T(8,128)(2,1)}), bf16[16,32,1536]{2,1,0:T(8,128)(2,1)S(1)}, u32[]{:S(2)}, u32[]{:S(2)}) async-start(bf16[16,32,1536]{2,1,0:T(8,128)(2,1)} %broadcast_in_dim.2), calls=%async_computation | async-start | bytes 3145728 | tf_op jit(solution)/shard_map/all_to_all | solution.py:115
  13.2 2.5 %collective-permute-start.1 = (bf16[768,768]{1,0:T(8,128)(2,1)S(1)}, bf16[768,768]{1,0:T(8,128)(2,1)}, u32[]{:S(2)}, u32[]{:S(2)}) collective-permute-start(bf16[768,768]{1,0:T(8,128)(2,1)S(1)} %copy-done), channel_id=1, source_target_pairs={{0,1},{1,0},{2,3},{3,2},{4,5},{5,4},{6,7},{7,6},{8,9},{9,8},{10,11... | collective-permute-start | bytes 3538952 | tf_op jit(solution)/shard_map/ppermute | solution.py:116
  15.7 18.8 %all_gather.3.first = bf16[128,768]{1,0:T(8,128)(2,1)S(1)} all-gather(bf16[32,768]{1,0:T(8,128)(2,1)S(1)} %copy-done.1), channel_id=1, replica_groups={{0,8,16,24},{2,10,18,26},{4,12,20,28},{6,14,22,30},{1,9,17,25},{3,11,19..., dimensions={0}, use_global_device_ids=true | all-gather | bytes 245760 | tf_op jit(solution)/shard_map/all_gather | solution.py:117
  34.6 4.6 %collective-permute-start.3 = (bf16[128,768]{1,0:T(8,128)(2,1)S(1)}, bf16[128,768]{1,0:T(8,128)(2,1)S(1)}, u32[]{:S(2)}, u32[]{:S(2)}) collective-permute-start(bf16[128,768]{1,0:T(8,128)(2,1)S(1)} %all_gather.3.first), channel_id=1, source_target_pairs={{0,4},{1,29},{2,6},{3,31},{4,8},{5,1},{6,10},{7,3},{8,12},{9,5},{1... | collective-permute-start | bytes 589832 | tf_op jit(solution)/shard_map/ppermute | solution.py:32
  39.2 0.0 all-to-all-done
  39.2 0.0 collective-permute-done.1.weight_other
  39.2 2.1 %shard_map.60 = bf16[256,768]{1,0:T(8,128)(2,1)S(1)} custom-call(s32[1]{0:T(128)} %bitcast.2.parity, bf16[8,2,32,1536]{3,2,1,0:T(8,128)(2,1)S(1)} %bitcast.5, bf16[768,768]{1,0:T(8,128)(2,1)S(1)} %copy-done, bf16[768,768]{1,0:T(8,128)(2,1)} %collective-permute-done.1.weight_other), custom_call_target="tpu_custom_call" | custom-call | flops 603979776 | bytes 1048576 | tf_op jit(solution)/shard_map/pallas_call | solution.py:40
  41.3 2.5 %collective-permute-start.2 = (bf16[256,768]{1,0:T(8,128)(2,1)S(1)}, bf16[256,768]{1,0:T(8,128)(2,1)S(1)}, u32[]{:S(2)}, u32[]{:S(2)}) collective-permute-start(bf16[256,768]{1,0:T(8,128)(2,1)S(1)} %shard_map.60), channel_id=1, source_target_pairs={{0,2},{1,31},{2,4},{3,1},{4,6},{5,3},{6,8},{7,5},{8,10},{9,7},{10,... | collective-permute-start | bytes 1179656 | tf_op jit(solution)/shard_map/ppermute | solution.py:32
  43.8 0.2 collective-permute-done.3.second
  44.0 5.0 %collective-permute-start.4 = (bf16[256,768]{1,0:T(8,128)(2,1)S(1)}, bf16[256,768]{1,0:T(8,128)(2,1)S(1)}, u32[]{:S(2)}, u32[]{:S(2)}) collective-permute-start(bf16[256,768]{1,0:T(8,128)(2,1)S(1)} %shard_map.63.refs_2_), channel_id=1, source_target_pairs={{0,30},{2,0},{4,2},{6,4},{8,6},{10,8},{12,10},{14,12},{16,14},{18,... | collective-permute-start | bytes 1179656 | tf_op jit(solution)/shard_map/ppermute | solution.py:36
  49.1 2.1 %shard_map.59.total = f32[256,768]{1,0:T(8,128)S(1)} custom-call(s32[1]{0:T(128)} %bitcast.parity, bf16[8,2,32,1536]{3,2,1,0:T(8,128)(2,1)S(1)} %bitcast.6, bf16[768,768]{1,0:T(8,128)(2,1)S(1)} %copy-done, bf16[768,768]{1,0:T(8,128)(2,1)} %collective-permute-done.1.weight_other), custom_call_target="tpu_custom_call" | custom-call | flops 603979776 | bytes 1048576 | tf_op jit(solution)/shard_map/pallas_call | solution.py:40
  51.2 0.8 shard_map.61
  52.0 10.7 %all-to-all-start.1 = ((bf16[8,32,768]{2,1,0:T(8,128)(2,1)}), bf16[8,32,768]{2,1,0:T(8,128)(2,1)S(1)}, u32[]{:S(2)}, u32[]{:S(2)}) async-start(bf16[8,32,768]{2,1,0:T(8,128)(2,1)} %shard_map.61), calls=%async_computation.1 | async-start | bytes 786432 | tf_op jit(solution)/shard_map/all_to_all | solution.py:142
  62.7 0.0 collective-permute-done.4.refs_3_
  62.7 0.8 shard_map.64
  63.5 5.9 %collective-permute-start.5 = (bf16[768,768]{1,0:T(8,128)(2,1)S(1)}, bf16[768,768]{1,0:T(8,128)(2,1)S(1)}, u32[]{:S(2)}, u32[]{:S(2)}) collective-permute-start(bf16[768,768]{1,0:T(8,128)(2,1)S(1)} %shard_map.64), channel_id=1, source_target_pairs={{0,1},{1,0},{2,3},{3,2},{4,5},{5,4},{6,7},{7,6},{8,9},{9,8},{10,11... | collective-permute-start | bytes 3538952 | tf_op jit(solution)/shard_map/ppermute | solution.py:153
  69.4 2.5 %collective-permute-done.5.refs_4_ = bf16[768,768]{1,0:T(8,128)(2,1)S(1)} collective-permute-done((bf16[768,768]{1,0:T(8,128)(2,1)S(1)}, bf16[768,768]{1,0:T(8,128)(2,1)S(1)}, u32[]{:S(2)}, u32[]{:S(2)}) %collective-permute-start.5) | collective-permute-done | bytes 1179680 | tf_op jit(solution)/shard_map/ppermute | solution.py:153
  71.9 1.8 %shard_map.65 = bf16[768,768]{1,0:T(8,128)(2,1)} custom-call(s32[1]{0:T(128)} %bitcast.3.refs_0_, bf16[4,4,32,1536]{3,2,1,0:T(8,128)(2,1)S(1)} %bitcast.8, bf16[256,768]{1,0:T(8,128)(2,1)S(1)} %shard_map.63.refs_2_, bf16[256,768]{1,0:T(8,128)(2,1)S(1)} %collective-permute-done.4.refs_3_, bf16[768,768]{1,0:T(8,128)(2,1)S(1)} %collective-permute-done.5.refs_4_), custom_call_target="tpu_custom_call" | custom-call | flops 1207959552 | bytes 1048576 | tf_op jit(solution)/shard_map/pallas_call | solution.py:40
  73.7 12.0 %all-to-all-done.1.parts = bf16[8,32,768]{2,1,0:T(8,128)(2,1)S(1)} async-done(((bf16[8,32,768]{2,1,0:T(8,128)(2,1)}), bf16[8,32,768]{2,1,0:T(8,128)(2,1)S(1)}, u32[]{:S(2)}, u32[]{:S(2)}) %all-to-all-start.1) | async-done | bytes 393248 | tf_op jit(solution)/shard_map/all_to_all | solution.py:142
  85.7 0.7 shard_map.62
  (8 shorter events, 0.0 us)
Async XLA Ops:
  1.5 3.5 %collective-permute-start = (bf16[32,768]{1,0:T(8,128)(2,1)S(1)}, bf16[32,768]{1,0:T(8,128)(2,1)S(1)}, u32[]{:S(2)}, u32[]{:S(2)}) collective-permute-start(bf16[32,768]{1,0:T(8,128)(2,1)S(1)} %fusion.15), channel_id=1, source_target_pairs={{0,1},{1,0},{2,3},{3,2},{4,5},{5,4},{6,7},{7,6},{8,9},{9,8},{10,11... | collective-permute-start | bytes 147464 | tf_op jit(solution)/shard_map/ppermute | solution.py:112
  6.3 6.9 %copy-start = (bf16[768,768]{1,0:T(8,128)(2,1)S(1)}, bf16[768,768]{1,0:T(8,128)(2,1)}, u32[]{:S(2)}) copy-start(bf16[768,768]{1,0:T(8,128)(2,1)} %weight.3) | copy-start | bytes 3538948
  6.3 9.4 %copy-start.1 = (bf16[32,768]{1,0:T(8,128)(2,1)S(1)}, bf16[32,768]{1,0:T(8,128)(2,1)}, u32[]{:S(2)}) copy-start(bf16[32,768]{1,0:T(8,128)(2,1)} %param.4) | copy-start | bytes 147460
  6.3 32.9 %all-to-all-start = ((bf16[16,32,1536]{2,1,0:T(8,128)(2,1)}), bf16[16,32,1536]{2,1,0:T(8,128)(2,1)S(1)}, u32[]{:S(2)}, u32[]{:S(2)}) async-start(bf16[16,32,1536]{2,1,0:T(8,128)(2,1)} %broadcast_in_dim.2), calls=%async_computation | async-start | bytes 3145728 | tf_op jit(solution)/shard_map/all_to_all | solution.py:115
  13.2 26.0 %collective-permute-start.1 = (bf16[768,768]{1,0:T(8,128)(2,1)S(1)}, bf16[768,768]{1,0:T(8,128)(2,1)}, u32[]{:S(2)}, u32[]{:S(2)}) collective-permute-start(bf16[768,768]{1,0:T(8,128)(2,1)S(1)} %copy-done), channel_id=1, source_target_pairs={{0,1},{1,0},{2,3},{3,2},{4,5},{5,4},{6,7},{7,6},{8,9},{9,8},{10,11... | collective-permute-start | bytes 3538952 | tf_op jit(solution)/shard_map/ppermute | solution.py:116
  34.6 9.4 %collective-permute-start.3 = (bf16[128,768]{1,0:T(8,128)(2,1)S(1)}, bf16[128,768]{1,0:T(8,128)(2,1)S(1)}, u32[]{:S(2)}, u32[]{:S(2)}) collective-permute-start(bf16[128,768]{1,0:T(8,128)(2,1)S(1)} %all_gather.3.first), channel_id=1, source_target_pairs={{0,4},{1,29},{2,6},{3,31},{4,8},{5,1},{6,10},{7,3},{8,12},{9,5},{1... | collective-permute-start | bytes 589832 | tf_op jit(solution)/shard_map/ppermute | solution.py:32
  41.3 9.9 %collective-permute-start.2 = (bf16[256,768]{1,0:T(8,128)(2,1)S(1)}, bf16[256,768]{1,0:T(8,128)(2,1)S(1)}, u32[]{:S(2)}, u32[]{:S(2)}) collective-permute-start(bf16[256,768]{1,0:T(8,128)(2,1)S(1)} %shard_map.60), channel_id=1, source_target_pairs={{0,2},{1,31},{2,4},{3,1},{4,6},{5,3},{6,8},{7,5},{8,10},{9,7},{10,... | collective-permute-start | bytes 1179656 | tf_op jit(solution)/shard_map/ppermute | solution.py:32
  44.0 18.6 %collective-permute-start.4 = (bf16[256,768]{1,0:T(8,128)(2,1)S(1)}, bf16[256,768]{1,0:T(8,128)(2,1)S(1)}, u32[]{:S(2)}, u32[]{:S(2)}) collective-permute-start(bf16[256,768]{1,0:T(8,128)(2,1)S(1)} %shard_map.63.refs_2_), channel_id=1, source_target_pairs={{0,30},{2,0},{4,2},{6,4},{8,6},{10,8},{12,10},{14,12},{16,14},{18,... | collective-permute-start | bytes 1179656 | tf_op jit(solution)/shard_map/ppermute | solution.py:36
  52.0 33.7 %all-to-all-start.1 = ((bf16[8,32,768]{2,1,0:T(8,128)(2,1)}), bf16[8,32,768]{2,1,0:T(8,128)(2,1)S(1)}, u32[]{:S(2)}, u32[]{:S(2)}) async-start(bf16[8,32,768]{2,1,0:T(8,128)(2,1)} %shard_map.61), calls=%async_computation.1 | async-start | bytes 786432 | tf_op jit(solution)/shard_map/all_to_all | solution.py:142
  63.5 8.4 %collective-permute-start.5 = (bf16[768,768]{1,0:T(8,128)(2,1)S(1)}, bf16[768,768]{1,0:T(8,128)(2,1)S(1)}, u32[]{:S(2)}, u32[]{:S(2)}) collective-permute-start(bf16[768,768]{1,0:T(8,128)(2,1)S(1)} %shard_map.64), channel_id=1, source_target_pairs={{0,1},{1,0},{2,3},{3,2},{4,5},{5,4},{6,7},{7,6},{8,9},{9,8},{10,11... | collective-permute-start | bytes 3538952 | tf_op jit(solution)/shard_map/ppermute | solution.py:153

commit v6 on v5

--- a/solution.py
+++ b/solution.py
@@ -30,10 +30,6 @@
         pairs.append((2 * z, 2 * ((z + step) % DEPTH)))
         pairs.append((2 * z + 1, 2 * ((z - step) % DEPTH) + 1))
     return lax.ppermute(x, ("z", "core"), pairs)
-
-
-def shift(x, step):
-    return lax.ppermute(x, "z", [(z, (z + step) % DEPTH) for z in range(DEPTH)])
 
 
 def call(kernel, out, *arrays, in_specs=None, out_specs=WHOLE, scratch_shapes=(), flops=1 << 20):
@@ -85,17 +81,17 @@
     out[...] = jnp.sum(parts[...].astype(jnp.float32), axis=0).astype(out.dtype)
 
 
-def for_other_kernel(scale, z, act, near, far, out):
+def for_other_kernel(scale, z, core, act, near, far, out):
     cols = slice(out.shape[1], None)
     total = dot(near[...], tokens_of(act, z[0], cols), 0, 0)
-    total = total + dot(far[...], tokens_of(act, z[0] + 1, cols), 0, 0)
+    total = total + dot(far[...], tokens_of(act, z[0] + 3 + 2 * core[0], cols), 0, 0)
     out[...] = (total * scale).astype(out.dtype)
 
 
-def own_kernel(scale, z, act, near, far, got, out):
+def own_kernel(scale, z, core, act, near, far, got, out):
     cols = slice(None, out.shape[1])
     total = dot(near[...], tokens_of(act, z[0], cols), 0, 0)
-    total = total + dot(far[...], tokens_of(act, z[0] + 1, cols), 0, 0)
+    total = total + dot(far[...], tokens_of(act, z[0] + 3 + 2 * core[0], cols), 0, 0)
     out[...] = (total * scale + got[...].astype(jnp.float32)).astype(out.dtype)
 
 
@@ -137,24 +133,24 @@
     far = products(1 - near, jnp.bfloat16)
     below = hop(far, 1)
     total = products(near, jnp.float32)
-    input_far = shift(after(input_near, far), -1)
+    input_far = hop(after(input_near, far), 1)
     sent = call(add_kernel, jax.ShapeDtypeStruct((DEPTH // 2, rows, half[1]), jnp.bfloat16), total, below)
     parts = lax.all_to_all(sent, "z", 0, 0, axis_index_groups=PARITIES, tiled=True)
     input_grad = call(sum_kernel, jax.ShapeDtypeStruct(inputs.shape, jnp.bfloat16), parts)
 
     act = arrived.reshape(4, 4, rows, 2 * width)
-    held = (z.reshape(1), act, input_near)
+    held = (z.reshape(1), core.reshape(1), act, input_near)
     for_other = call(
         lambda *refs: for_other_kernel(scale, *refs),
         square, *held, after(input_far, sent),
-        in_specs=[scalars] + [WHOLE] * 3,
+        in_specs=[scalars] * 2 + [WHOLE] * 3,
         flops=2 * flops,
     )
     got = lax.ppermute(for_other, "core", SWAP)
     weight_grad = call(
         lambda *refs: own_kernel(scale, *refs),
         square, *held, input_far, got,
-        in_specs=[scalars] + [WHOLE] * 4,
+        in_specs=[scalars] * 2 + [WHOLE] * 4,
         flops=2 * flops,
     )
     return input_grad, weight_grad

time: 87 us -> 87.1 us (level)
  the two profiles are of different devices: /device:TPU:129 before, /device:TPU:64 now
where the time goes in v6:
time: 87.1 us; the launch traced here: 86.4 us
  starting transfers between devices  33.2 us (38%)
  blocking collectives  25.5 us (29%)
  waiting for transfers between devices  15.6 us (18%)
  Pallas kernels  8.29 us (10%)
  other arithmetic  1.77 us (2%)
  local copies, waits for them, and re-layouts  1.31 us (2%)
    all_gather x1, blocking collectives, on_device(): lax.all_gather(after(inputs, copies), 'z', axis=0, axis_index_groups=QUAR...  25.5 us
    all_to_all x1, waiting for transfers between devices, on_device(): lax.all_to_all(sent, 'z', 0, 0, axis_index_groups=PARITIES, tiled=True)  11.5 us
    ppermute x3, starting transfers between devices, hop(): return lax.ppermute(x, ('z', 'core'), pairs)  10.5 us
    all_to_all x1, starting transfers between devices, on_device(): lax.all_to_all(sent, 'z', 0, 0, axis_index_groups=PARITIES, tiled=True)  9.77 us
    pallas_call x7, Pallas kernels, call(): pl.pallas_call(kernel, out_shape=out, in_specs=in_specs or [WHOLE] * len(...  8.29 us
    all_to_all x1, starting transfers between devices, on_device(): arrived = lax.all_to_all(copies, ('y', 'x'), 0, 0, tiled=True)  7.17 us
    ppermute x1, waiting for transfers between devices, on_device(): got = lax.ppermute(for_other, 'core', SWAP)  2.81 us
    ppermute x1, starting transfers between devices, on_device(): weight_other = lax.ppermute(after(weight, copies), 'core', SWAP)  1.92 us
  transfers between devices with their start and end apart: 8, of which 5 were waited for; matrix products, arithmetic and copies ran while one was open for 1% of the time, Pallas kernels for 9%

profile of v6, /device:TPU:64, one launch (start us, length us, event | category | flops | bytes accessed | tf_op | source)
XLA Modules:
  0.0 86.4 jit_solution(12436442960791286762)
XLA Ops:
  0.6 0.9 %fusion.15 = bf16[32,768]{1,0:T(8,128)(2,1)S(1)} fusion(bf16[64,768]{1,0:T(8,128)(2,1)} %param.6, s32[]{:T(128)S(6)} %select_n.16, bf16[64,768]{1,0:T(8,128)(2,1)} %param.5), kind=kLoop, calls=%fused_computation.24 | loop fusion | flops 294912 | bytes 147460 | tf_op jit(solution)/shard_map/convert_element_type | solution.py:20
  1.5 1.9 %collective-permute-start = (bf16[32,768]{1,0:T(8,128)(2,1)S(1)}, bf16[32,768]{1,0:T(8,128)(2,1)S(1)}, u32[]{:S(2)}, u32[]{:S(2)}) collective-permute-start(bf16[32,768]{1,0:T(8,128)(2,1)S(1)} %fusion.15), channel_id=1, source_target_pairs={{0,1},{1,0},{2,3},{3,2},{4,5},{5,4},{6,7},{7,6},{8,9},{9,8},{10,11... | collective-permute-start | bytes 147464 | tf_op jit(solution)/shard_map/ppermute | solution.py:108
  3.5 0.9 %fusion.14 = bf16[32,768]{1,0:T(8,128)(2,1)S(1)} fusion(bf16[64,768]{1,0:T(8,128)(2,1)} %param.6, s32[]{:T(128)S(6)} %select_n.17, bf16[64,768]{1,0:T(8,128)(2,1)} %param.5), kind=kLoop, calls=%fused_computation.23 | loop fusion | flops 294912 | bytes 147460 | tf_op jit(solution)/shard_map/convert_element_type | solution.py:20
  4.3 0.3 collective-permute-done
  4.7 1.3 %broadcast_in_dim.2 = bf16[16,32,1536]{2,1,0:T(8,128)(2,1)} broadcast(bf16[32,1536]{1,0:T(8,128)(2,1)S(1)} %pad_maximum_fusion), dimensions={1,2} | broadcast | bytes 1671168 | tf_op jit(solution)/shard_map/broadcast_in_dim | solution.py:110
  6.0 7.2 %all-to-all-start = ((bf16[16,32,1536]{2,1,0:T(8,128)(2,1)}), bf16[16,32,1536]{2,1,0:T(8,128)(2,1)S(1)}, u32[]{:S(2)}, u32[]{:S(2)}) async-start(bf16[16,32,1536]{2,1,0:T(8,128)(2,1)} %broadcast_in_dim.2), calls=%async_computation | async-start | bytes 3145728 | tf_op jit(solution)/shard_map/all_to_all | solution.py:111
  13.1 1.9 %collective-permute-start.1 = (bf16[768,768]{1,0:T(8,128)(2,1)S(1)}, bf16[768,768]{1,0:T(8,128)(2,1)}, u32[]{:S(2)}, u32[]{:S(2)}) collective-permute-start(bf16[768,768]{1,0:T(8,128)(2,1)S(1)} %copy-done), channel_id=1, source_target_pairs={{0,1},{1,0},{2,3},{3,2},{4,5},{5,4},{6,7},{7,6},{8,9},{9,8},{10,11... | collective-permute-start | bytes 3538952 | tf_op jit(solution)/shard_map/ppermute | solution.py:112
  15.1 25.5 %all_gather.3.first = bf16[128,768]{1,0:T(8,128)(2,1)S(1)} all-gather(bf16[32,768]{1,0:T(8,128)(2,1)S(1)} %copy-done.1), channel_id=1, replica_groups={{0,8,16,24},{2,10,18,26},{4,12,20,28},{6,14,22,30},{1,9,17,25},{3,11,19..., dimensions={0}, use_global_device_ids=true | all-gather | bytes 245760 | tf_op jit(solution)/shard_map/all_gather | solution.py:113
  40.6 4.0 %collective-permute-start.3 = (bf16[128,768]{1,0:T(8,128)(2,1)S(1)}, bf16[128,768]{1,0:T(8,128)(2,1)S(1)}, u32[]{:S(2)}, u32[]{:S(2)}) collective-permute-start(bf16[128,768]{1,0:T(8,128)(2,1)S(1)} %all_gather.3.first), channel_id=1, source_target_pairs={{0,4},{1,29},{2,6},{3,31},{4,8},{5,1},{6,10},{7,3},{8,12},{9,5},{1... | collective-permute-start | bytes 589832 | tf_op jit(solution)/shard_map/ppermute | solution.py:32
  44.6 0.0 all-to-all-done
  44.6 2.1 %shard_map.60 = bf16[256,768]{1,0:T(8,128)(2,1)S(1)} custom-call(s32[1]{0:T(128)} %bitcast.2.parity, bf16[8,2,32,1536]{3,2,1,0:T(8,128)(2,1)S(1)} %bitcast.6, bf16[768,768]{1,0:T(8,128)(2,1)S(1)} %copy-done, bf16[768,768]{1,0:T(8,128)(2,1)} %collective-permute-done.1.weight_other), custom_call_target="tpu_custom_call" | custom-call | flops 603979776 | bytes 1048576 | tf_op jit(solution)/shard_map/pallas_call | solution.py:36
  46.7 2.3 %collective-permute-start.2 = (bf16[256,768]{1,0:T(8,128)(2,1)S(1)}, bf16[256,768]{1,0:T(8,128)(2,1)S(1)}, u32[]{:S(2)}, u32[]{:S(2)}) collective-permute-start(bf16[256,768]{1,0:T(8,128)(2,1)S(1)} %shard_map.60), channel_id=1, source_target_pairs={{0,2},{1,31},{2,4},{3,1},{4,6},{5,3},{6,8},{7,5},{8,10},{9,7},{10,... | collective-permute-start | bytes 1179656 | tf_op jit(solution)/shard_map/ppermute | solution.py:32
  48.9 0.8 collective-permute-done.3.second
  49.7 4.3 %collective-permute-start.4 = (bf16[256,768]{1,0:T(8,128)(2,1)S(1)}, bf16[256,768]{1,0:T(8,128)(2,1)S(1)}, u32[]{:S(2)}, u32[]{:S(2)}) collective-permute-start(bf16[256,768]{1,0:T(8,128)(2,1)S(1)} %shard_map.63.refs_3_), channel_id=1, source_target_pairs={{0,2},{1,31},{2,4},{3,1},{4,6},{5,3},{6,8},{7,5},{8,10},{9,7},{10,... | collective-permute-start | bytes 1179656 | tf_op jit(solution)/shard_map/ppermute | solution.py:32
  54.1 2.1 %shard_map.59.total = f32[256,768]{1,0:T(8,128)S(1)} custom-call(s32[1]{0:T(128)} %bitcast.parity, bf16[8,2,32,1536]{3,2,1,0:T(8,128)(2,1)S(1)} %bitcast.7, bf16[768,768]{1,0:T(8,128)(2,1)S(1)} %copy-done, bf16[768,768]{1,0:T(8,128)(2,1)} %collective-permute-done.1.weight_other), custom_call_target="tpu_custom_call" | custom-call | flops 603979776 | bytes 1048576 | tf_op jit(solution)/shard_map/pallas_call | solution.py:36
  56.1 0.2 collective-permute-done.2.below
  56.3 0.8 shard_map.61
  57.1 9.8 %all-to-all-start.1 = ((bf16[8,32,768]{2,1,0:T(8,128)(2,1)}), bf16[8,32,768]{2,1,0:T(8,128)(2,1)S(1)}, u32[]{:S(2)}, u32[]{:S(2)}) async-start(bf16[8,32,768]{2,1,0:T(8,128)(2,1)} %shard_map.61), calls=%async_computation.1 | async-start | bytes 786432 | tf_op jit(solution)/shard_map/all_to_all | solution.py:138
  66.9 0.8 shard_map.64
  67.7 1.9 %collective-permute-start.5 = (bf16[768,768]{1,0:T(8,128)(2,1)S(1)}, bf16[768,768]{1,0:T(8,128)(2,1)S(1)}, u32[]{:S(2)}, u32[]{:S(2)}) collective-permute-start(bf16[768,768]{1,0:T(8,128)(2,1)S(1)} %shard_map.64), channel_id=1, source_target_pairs={{0,1},{1,0},{2,3},{3,2},{4,5},{5,4},{6,7},{7,6},{8,9},{9,8},{10,11... | collective-permute-start | bytes 3538952 | tf_op jit(solution)/shard_map/ppermute | solution.py:149
  69.7 2.8 %collective-permute-done.5.refs_5_ = bf16[768,768]{1,0:T(8,128)(2,1)S(1)} collective-permute-done((bf16[768,768]{1,0:T(8,128)(2,1)S(1)}, bf16[768,768]{1,0:T(8,128)(2,1)S(1)}, u32[]{:S(2)}, u32[]{:S(2)}) %collective-permute-start.5) | collective-permute-done | bytes 1179680 | tf_op jit(solution)/shard_map/ppermute | solution.py:149
  72.5 1.8 %shard_map.65 = bf16[768,768]{1,0:T(8,128)(2,1)} custom-call(s32[1]{0:T(128)} %bitcast.3.refs_0_, s32[1]{0:T(128)} %bitcast.4.refs_1_, bf16[4,4,32,1536]{3,2,1,0:T(8,128)(2,1)S(1)} %bitcast.9, bf16[256,768]{1,0:T(8,128)(2,1)S(1)} %shard_map.63.refs_3_, bf16[256,768]{1,0:T(8,128)(2,1)S(1)} %collective-permute-done.4.refs_4_, ...), custom_call_target="tpu_custom_call" | custom-call | flops 1207959552 | bytes 1048576 | tf_op jit(solution)/shard_map/pallas_call | solution.py:36
  74.3 11.5 %all-to-all-done.1.parts = bf16[8,32,768]{2,1,0:T(8,128)(2,1)S(1)} async-done(((bf16[8,32,768]{2,1,0:T(8,128)(2,1)}), bf16[8,32,768]{2,1,0:T(8,128)(2,1)S(1)}, u32[]{:S(2)}, u32[]{:S(2)}) %all-to-all-start.1) | async-done | bytes 393248 | tf_op jit(solution)/shard_map/all_to_all | solution.py:138
  85.8 0.7 shard_map.62
  (8 shorter events, 0.0 us)
Async XLA Ops:
  1.5 3.1 %collective-permute-start = (bf16[32,768]{1,0:T(8,128)(2,1)S(1)}, bf16[32,768]{1,0:T(8,128)(2,1)S(1)}, u32[]{:S(2)}, u32[]{:S(2)}) collective-permute-start(bf16[32,768]{1,0:T(8,128)(2,1)S(1)} %fusion.15), channel_id=1, source_target_pairs={{0,1},{1,0},{2,3},{3,2},{4,5},{5,4},{6,7},{7,6},{8,9},{9,8},{10,11... | collective-permute-start | bytes 147464 | tf_op jit(solution)/shard_map/ppermute | solution.py:108
  6.0 7.2 %copy-start = (bf16[768,768]{1,0:T(8,128)(2,1)S(1)}, bf16[768,768]{1,0:T(8,128)(2,1)}, u32[]{:S(2)}) copy-start(bf16[768,768]{1,0:T(8,128)(2,1)} %weight.3) | copy-start | bytes 3538948
  6.0 9.1 %copy-start.1 = (bf16[32,768]{1,0:T(8,128)(2,1)S(1)}, bf16[32,768]{1,0:T(8,128)(2,1)}, u32[]{:S(2)}) copy-start(bf16[32,768]{1,0:T(8,128)(2,1)} %param.4) | copy-start | bytes 147460
  6.0 38.6 %all-to-all-start = ((bf16[16,32,1536]{2,1,0:T(8,128)(2,1)}), bf16[16,32,1536]{2,1,0:T(8,128)(2,1)S(1)}, u32[]{:S(2)}, u32[]{:S(2)}) async-start(bf16[16,32,1536]{2,1,0:T(8,128)(2,1)} %broadcast_in_dim.2), calls=%async_computation | async-start | bytes 3145728 | tf_op jit(solution)/shard_map/all_to_all | solution.py:111
  13.1 31.4 %collective-permute-start.1 = (bf16[768,768]{1,0:T(8,128)(2,1)S(1)}, bf16[768,768]{1,0:T(8,128)(2,1)}, u32[]{:S(2)}, u32[]{:S(2)}) collective-permute-start(bf16[768,768]{1,0:T(8,128)(2,1)S(1)} %copy-done), channel_id=1, source_target_pairs={{0,1},{1,0},{2,3},{3,2},{4,5},{5,4},{6,7},{7,6},{8,9},{9,8},{10,11... | collective-permute-start | bytes 3538952 | tf_op jit(solution)/shard_map/ppermute | solution.py:112
  40.6 9.1 %collective-permute-start.3 = (bf16[128,768]{1,0:T(8,128)(2,1)S(1)}, bf16[128,768]{1,0:T(8,128)(2,1)S(1)}, u32[]{:S(2)}, u32[]{:S(2)}) collective-permute-start(bf16[128,768]{1,0:T(8,128)(2,1)S(1)} %all_gather.3.first), channel_id=1, source_target_pairs={{0,4},{1,29},{2,6},{3,31},{4,8},{5,1},{6,10},{7,3},{8,12},{9,5},{1... | collective-permute-start | bytes 589832 | tf_op jit(solution)/shard_map/ppermute | solution.py:32
  46.7 9.7 %collective-permute-start.2 = (bf16[256,768]{1,0:T(8,128)(2,1)S(1)}, bf16[256,768]{1,0:T(8,128)(2,1)S(1)}, u32[]{:S(2)}, u32[]{:S(2)}) collective-permute-start(bf16[256,768]{1,0:T(8,128)(2,1)S(1)} %shard_map.60), channel_id=1, source_target_pairs={{0,2},{1,31},{2,4},{3,1},{4,6},{5,3},{6,8},{7,5},{8,10},{9,7},{10,... | collective-permute-start | bytes 1179656 | tf_op jit(solution)/shard_map/ppermute | solution.py:32
  49.7 17.2 %collective-permute-start.4 = (bf16[256,768]{1,0:T(8,128)(2,1)S(1)}, bf16[256,768]{1,0:T(8,128)(2,1)S(1)}, u32[]{:S(2)}, u32[]{:S(2)}) collective-permute-start(bf16[256,768]{1,0:T(8,128)(2,1)S(1)} %shard_map.63.refs_3_), channel_id=1, source_target_pairs={{0,2},{1,31},{2,4},{3,1},{4,6},{5,3},{6,8},{7,5},{8,10},{9,7},{10,... | collective-permute-start | bytes 1179656 | tf_op jit(solution)/shard_map/ppermute | solution.py:32
  57.1 28.6 %all-to-all-start.1 = ((bf16[8,32,768]{2,1,0:T(8,128)(2,1)}), bf16[8,32,768]{2,1,0:T(8,128)(2,1)S(1)}, u32[]{:S(2)}, u32[]{:S(2)}) async-start(bf16[8,32,768]{2,1,0:T(8,128)(2,1)} %shard_map.61), calls=%async_computation.1 | async-start | bytes 786432 | tf_op jit(solution)/shard_map/all_to_all | solution.py:138
  67.7 4.7 %collective-permute-start.5 = (bf16[768,768]{1,0:T(8,128)(2,1)S(1)}, bf16[768,768]{1,0:T(8,128)(2,1)S(1)}, u32[]{:S(2)}, u32[]{:S(2)}) collective-permute-start(bf16[768,768]{1,0:T(8,128)(2,1)S(1)} %shard_map.64), channel_id=1, source_target_pairs={{0,1},{1,0},{2,3},{3,2},{4,5},{5,4},{6,7},{7,6},{8,9},{9,8},{10,11... | collective-permute-start | bytes 3538952 | tf_op jit(solution)/shard_map/ppermute | solution.py:149
